TPU v7x, 512 devices: a whole 4x8x8 slice. The times are simulated.
512 devices in a mesh: learn: 32 (over z, y_lo, core), roll: 16 (over y_hi, x).
Axes of the slice: x: 4, y: 8 (y_hi: 4, y_lo: 2; y = y_hi * 2 + y_lo), z: 8, core: 2. Of those that a mesh axis runs over, the one named last changes fastest.
Arguments:
- frozen_weight: bfloat16 [8192, 28672], P('roll', 'learn'), may hold values from -0.00048828125 to 0.00048828125
- projection_inputs: bfloat16 [20480, 28672], P('learn', 'roll'), may hold values from -6 to 6
- output_gradients: bfloat16 [20480, 8192], P('learn', 'roll'), may hold values from -6 to 6
- adapter_down_factor: float32 [128, 28672], P('learn', 'roll'), may hold values from -0.01953125 to 0.01953125
- down_first_moment: float32 [128, 28672], P('learn', 'roll'), may hold values from -0.5 to 0.5
- down_second_moment: float32 [128, 28672], P('learn', 'roll'), may hold values from 0.0006 to 0.01
- adapter_up_factor: float32 [128, 8192], P('learn', 'roll'), may hold values from -0.01171875 to 0.01171875
- up_first_moment: float32 [128, 8192], P('learn', 'roll'), may hold values from -1.5 to 1.5
- up_second_moment: float32 [128, 8192], P('learn', 'roll'), may hold values from 0.006 to 0.1
Outputs:
- weight_with_adapter: bfloat16 [8192, 28672], P('roll', 'learn')
- down_factor_updated: float32 [128, 28672], P('learn', 'roll')
- down_first_updated: float32 [128, 28672], P('learn', 'roll')
- down_second_updated: float32 [128, 28672], P('learn', 'roll')
- up_factor_updated: float32 [128, 8192], P('learn', 'roll')
- up_first_updated: float32 [128, 8192], P('learn', 'roll')
- up_second_updated: float32 [128, 8192], P('learn', 'roll')
All inputs are finite; a program needn't handle non-finite values.
Results may differ from a plain program's by a relative error of at most 0.018.
Values may be sent and summed in bfloat16 or wider, within the bound.
A program may use at most 64 MiB of HBM per device.

v0:
```python
import math

import jax
import jax.numpy as jnp
from jax import lax
from jax.sharding import PartitionSpec as P

ADAPTER_RANK = 128
STEP = 20


adapter_scale = 2.0
learning_rate = 0.001
beta_one = 0.9
beta_two = 0.999
epsilon = 1e-08
weight_decay = 0.01


def contraction_rows(left, right):
    return lax.dot_general(
        left, right, (((0,), (0,)), ((), ())), preferred_element_type=jnp.float32
    )


def contract_cols(left, right):
    return lax.dot_general(
        left, right, (((1,), (1,)), ((), ())), preferred_element_type=jnp.float32
    )


def decoupled_adam_update(weights, moment_one, moment_two, gradient):
    one_next = beta_one * moment_one + (1.0 - beta_one) * gradient
    two_next = beta_two * moment_two + (1.0 - beta_two) * gradient * gradient
    corr_one = 1.0 - beta_one**STEP
    corr_two = 1.0 - beta_two**STEP
    update = one_next / corr_one / (jnp.sqrt(two_next / corr_two) + epsilon)
    return (weights - learning_rate * (update + weight_decay * weights), one_next, two_next)


def per_device(
    frozen_weight,
    projection_inputs,
    output_gradients,
    adapter_down_factor,
    down_first_moment,
    down_second_moment,
    adapter_up_factor,
    up_first_moment,
    up_second_moment,
):
    learners = lax.axis_size("learn")
    learn_index = lax.axis_index("learn")
    down_rows, up_rows = (
        lax.all_gather(adapter_down_factor.astype(jnp.bfloat16), "learn", axis=0, tiled=True),
        lax.all_gather(adapter_up_factor.astype(jnp.bfloat16), "learn", axis=0, tiled=True),
    )
    hidden_part = contract_cols(projection_inputs, down_rows)
    back_part = contract_cols(output_gradients, up_rows)
    hidden_sum, backward_total = lax.psum((hidden_part, back_part), "roll")
    hidden_low_rank = hidden_sum.astype(jnp.bfloat16)
    backward_low_rank = (adapter_scale * backward_total).astype(jnp.bfloat16)
    normalizer_scale = 1.0 / math.sqrt(projection_inputs.shape[0] * learners)
    owned_count = ADAPTER_RANK // learners
    left_part = normalizer_scale * contraction_rows(backward_low_rank, projection_inputs)
    right_operand = (
        adapter_scale * normalizer_scale * contraction_rows(hidden_low_rank, output_gradients)
    )
    summed = lax.psum(
        jnp.concatenate([left_part, right_operand], axis=1).astype(jnp.bfloat16), "learn"
    ).astype(jnp.float32)
    local_gradients = lax.dynamic_slice_in_dim(summed, learn_index * owned_count, owned_count, 0)
    down_factor_width = adapter_down_factor.shape[1]
    down_factor_updated, down_first_updated, down_second_updated = decoupled_adam_update(
        adapter_down_factor,
        down_first_moment,
        down_second_moment,
        local_gradients[:, :down_factor_width],
    )
    up_factor_updated, up_first_updated, up_second_updated = decoupled_adam_update(
        adapter_up_factor, up_first_moment, up_second_moment, local_gradients[:, down_factor_width:]
    )
    rank_rows = lax.all_gather(
        down_factor_updated.astype(jnp.bfloat16), "learn", axis=0, tiled=True
    )
    block_width = frozen_weight.shape[1]
    every_column = lax.all_gather(rank_rows, "roll", axis=1, tiled=True)
    down_factor_block = lax.dynamic_slice_in_dim(
        every_column, learn_index * block_width, block_width, 1
    )
    up_rounded = up_factor_updated.astype(jnp.bfloat16)
    rank_entries = lax.all_gather(up_rounded, "learn", axis=0, tiled=True)
    combined_weight = frozen_weight.astype(jnp.float32) + adapter_scale * contraction_rows(
        rank_entries, down_factor_block
    )
    weight_with_adapter = combined_weight.astype(jnp.bfloat16)
    return (
        weight_with_adapter,
        down_factor_updated,
        down_first_updated,
        down_second_updated,
        up_factor_updated,
        up_first_updated,
        up_second_updated,
    )


def solution(mesh):
    placed = (
        P("roll", "learn"),
        P("learn", "roll"),
        P("learn", "roll"),
        P("learn", "roll"),
        P("learn", "roll"),
        P("learn", "roll"),
        P("learn", "roll"),
        P("learn", "roll"),
        P("learn", "roll"),
    )
    return jax.shard_map(
        per_device,
        mesh=mesh,
        in_specs=placed,
        out_specs=(
            P("roll", "learn"),
            P("learn", "roll"),
            P("learn", "roll"),
            P("learn", "roll"),
            P("learn", "roll"),
            P("learn", "roll"),
            P("learn", "roll"),
        ),
        check_vma=False,
    )
```

profile of v0, /device:TPU:1, one launch (start us, length us, event | category | flops | bytes accessed | tf_op | source)
XLA Modules:
  0.0 590.3 jit_solution(5313417742716080359)
XLA Ops:
  7.2 0.0 copy-start
  7.2 0.0 all-reduce.4.cloned.1.call-start
  7.2 0.9 convert_bitcast_fusion.3
  8.1 42.2 %all-gather = bf16[32,4,512]{2,1,0:T(4,128)(2,1)S(1)} all-gather(bf16[1,4,512]{2,1,0:T(4,128)(2,1)S(1)} %convert_bitcast_fusion.3), channel_id=1, replica_groups=mesh['learn'=32,'roll'=16] {'learn'}, dimensions={0}, use_global_device_ids=true | all-gather | bytes 135168 | tf_op jit(solution)/shard_map/all_gather | solution.py:56
  50.4 2.1 fusion.11
  52.5 0.0 all-reduce.4.cloned.1.call-update
  52.5 0.0 all-reduce.6.cloned.1.call-start
  52.6 0.8 convert_bitcast_fusion.1
  53.3 32.6 %all-gather.1 = bf16[32,4,1792]{2,1,0:T(4,128)(2,1)S(1)} all-gather(bf16[1,4,1792]{2,1,0:T(4,128)(2,1)S(1)} %convert_bitcast_fusion.1), channel_id=1, replica_groups=mesh['learn'=32,'roll'=16] {'learn'}, dimensions={0}, use_global_device_ids=true | all-gather | bytes 473088 | tf_op jit(solution)/shard_map/all_gather | solution.py:55
  85.9 0.9 reshape.17
  86.8 0.0 copy-done
  86.8 0.0 copy-start.1
  86.8 1.8 fusion.12
  88.6 72.3 %all-reduce.7 = bf16[640,128]{1,0:T(8,128)(2,1)S(1)} all-reduce(f32[640,128]{1,0:T(8,128)S(1)} %fusion.12), channel_id=1, replica_groups=mesh['learn'=32,'roll'=16] {'roll'}, use_global_device_ids=true, to_apply=%region_1.0 | all-reduce | flops 81920 | bytes 491520 | tf_op jit(solution)/shard_map/psum | solution.py:60
  160.9 0.0 copy-done.1
  160.9 0.3 fusion.1
  161.2 0.0 copy-start.2
  161.2 0.0 copy-start.4
  161.3 0.0 copy-start.5
  161.3 42.8 %all-reduce.4.cloned.1.call-done = f32[640,128]{1,0:T(8,128)} async-done(((f32[640,128]{1,0:T(8,128)}), f32[640,128]{1,0:T(8,128)}) %all-reduce.4.cloned.1.call-update) | async-done | bytes 327696 | tf_op jit(solution)/shard_map/psum | solution.py:60
  204.1 1.5 fusion
  205.6 0.0 copy-start.3
  205.6 0.0 copy-start.6
  205.7 0.0 copy-start.7
  205.7 0.9 pad_maximum_fusion
  206.5 0.0 all-reduce.6.cloned.1.call-update
  206.5 0.0 all-gather.6.cloned.1.call-start
  206.6 230.4 %all-reduce.6.cloned.1.call-done = bf16[128,2304]{1,0:T(8,128)(2,1)} async-done(((bf16[128,2304]{1,0:T(8,128)(2,1)}), bf16[128,2304]{1,0:T(8,128)(2,1)}) %all-reduce.6.cloned.1.call-update) | async-done | bytes 589840 | tf_op jit(solution)/shard_map/psum | solution.py:69
  437.0 0.8 dynamic-slice_convert_fusion
  437.7 0.0 copy-done.2
  437.7 0.0 copy-done.4
  437.8 0.0 copy-done.5
  437.8 0.7 convert_bitcast_fusion
  438.4 34.8 %all-gather.3 = bf16[32,4,1792]{2,1,0:T(4,128)(2,1)S(1)} all-gather(bf16[1,4,1792]{2,1,0:T(4,128)(2,1)S(1)} %get-tuple-element.7), channel_id=1, replica_groups=mesh['learn'=32,'roll'=16] {'learn'}, dimensions={0}, use_global_device_ids=true | all-gather | bytes 473088 | tf_op jit(solution)/shard_map/all_gather | solution.py:83
  473.3 0.9 reshape.21
  474.2 0.0 all-gather.6.cloned.1.call-update
  474.2 0.0 copy-done.3
  474.2 0.0 copy-done.6
  474.2 0.0 copy-done.7
  474.2 0.6 convert_bitcast_fusion.2
  474.8 34.3 %all-gather.2 = bf16[32,4,512]{2,1,0:T(4,128)(2,1)S(1)} all-gather(bf16[1,4,512]{2,1,0:T(4,128)(2,1)S(1)} %get-tuple-element.11), channel_id=1, replica_groups=mesh['learn'=32,'roll'=16] {'learn'}, dimensions={0}, use_global_device_ids=true | all-gather | bytes 135168 | tf_op jit(solution)/shard_map/all_gather | solution.py:92
  509.1 72.0 %all-gather.6.cloned.1.call-done = bf16[128,28672]{1,0:T(8,128)(2,1)} async-done(((bf16[128,1792]{1,0:T(8,128)(2,1)}), bf16[128,28672]{1,0:T(8,128)(2,1)}) %all-gather.6.cloned.1.call-update) | async-done | bytes 7340048 | tf_op jit(solution)/shard_map/all_gather | solution.py:87
  581.2 2.7 add_convert_fusion
  (2 shorter events, 0.1 us)
Async XLA Ops:
  7.2 79.6 %copy-start = (bf16[640,1792]{1,0:T(8,128)(2,1)S(1)}, bf16[640,1792]{1,0:T(8,128)(2,1)}, u32[]{:S(2)}) copy-start(bf16[640,1792]{1,0:T(8,128)(2,1)} %param.10) | copy-start | bytes 6881284
  7.2 196.9 %all-reduce.4.cloned.1.call-start = ((), (), s32[]{:S(2)}) async-start(), calls=%async_computation | async-start | bytes 655360 | tf_op jit(solution)/shard_map/psum | solution.py:60
  52.5 384.4 %all-reduce.6.cloned.1.call-start = ((), (), s32[]{:S(2)}) async-start(), calls=%async_computation.1 | async-start | bytes 1179648 | tf_op jit(solution)/shard_map/psum | solution.py:69
  86.8 74.1 %copy-start.1 = (bf16[640,512]{1,0:T(8,128)(2,1)S(1)}, bf16[640,512]{1,0:T(8,128)(2,1)}, u32[]{:S(2)}) copy-start(bf16[640,512]{1,0:T(8,128)(2,1)} %param.11) | copy-start | bytes 1966084
  161.2 276.5 %copy-start.2 = (f32[4,1792]{1,0:T(4,128)S(1)}, f32[4,1792]{1,0:T(4,128)}, u32[]{:S(2)}) copy-start(f32[4,1792]{1,0:T(4,128)} %param.12) | copy-start | bytes 86020
  161.2 276.5 %copy-start.4 = (f32[4,1792]{1,0:T(4,128)S(1)}, f32[4,1792]{1,0:T(4,128)}, u32[]{:S(2)}) copy-start(f32[4,1792]{1,0:T(4,128)} %param.13) | copy-start | bytes 86020
  161.3 276.5 %copy-start.5 = (f32[4,1792]{1,0:T(4,128)S(1)}, f32[4,1792]{1,0:T(4,128)}, u32[]{:S(2)}) copy-start(f32[4,1792]{1,0:T(4,128)} %param.14) | copy-start | bytes 86020
  205.6 268.6 %copy-start.3 = (f32[4,512]{1,0:T(4,128)S(1)}, f32[4,512]{1,0:T(4,128)}, u32[]{:S(2)}) copy-start(f32[4,512]{1,0:T(4,128)} %param.15) | copy-start | bytes 24580
  205.6 268.5 %copy-start.6 = (f32[4,512]{1,0:T(4,128)S(1)}, f32[4,512]{1,0:T(4,128)}, u32[]{:S(2)}) copy-start(f32[4,512]{1,0:T(4,128)} %param.16) | copy-start | bytes 24580
  205.7 268.5 %copy-start.7 = (f32[4,512]{1,0:T(4,128)S(1)}, f32[4,512]{1,0:T(4,128)}, u32[]{:S(2)}) copy-start(f32[4,512]{1,0:T(4,128)} %param.17) | copy-start | bytes 24580
  206.5 374.6 %all-gather.6.cloned.1.call-start = ((), (), s32[]{:S(2)}) async-start(), calls=%async_computation.2 | async-start | bytes 7798784 | tf_op jit(solution)/shard_map/all_gather | solution.py:87
Sparse Core Ops, SparseCore 0:
  52.6 151.4 all-reduce.3
  207.8 229.0 all-reduce.5
  474.3 106.8 all-gather.5
where the time goes:
time: 596 us; the launch traced here: 590 us
  waiting for transfers between devices  345 us (58%)
  blocking collectives  216 us (36%)
  between operations  13.9 us (2%)
  matrix products  8.46 us (1%)
    psum x1, waiting for transfers between devices, per_device(): lax.psum(jnp.concatenate([left_part, right_operand], axis=1).astype(jnp.b...  230 us
    psum x1, blocking collectives, per_device(): hidden_sum, backward_total = lax.psum((hidden_part, back_part), 'roll')  72.3 us
    all_gather x1, waiting for transfers between devices, per_device(): every_column = lax.all_gather(rank_rows, 'roll', axis=1, tiled=True)  72 us
    psum x1, waiting for transfers between devices, per_device(): hidden_sum, backward_total = lax.psum((hidden_part, back_part), 'roll')  42.8 us
    all_gather x1, blocking collectives, per_device(): lax.all_gather(adapter_up_factor.astype(jnp.bfloat16), 'learn', axis=0, t...  42.2 us
    all_gather x1, blocking collectives, per_device(): lax.all_gather(down_factor_updated.astype(jnp.bfloat16), 'learn', axis=0,...  34.8 us
    all_gather x1, blocking collectives, per_device(): rank_entries = lax.all_gather(up_rounded, 'learn', axis=0, tiled=True)  34.3 us
    all_gather x1, blocking collectives, per_device(): lax.all_gather(adapter_down_factor.astype(jnp.bfloat16), 'learn', axis=0,...  32.6 us
  transfers between devices with their start and end apart: 3, of which 3 were waited for; matrix products, arithmetic and copies ran while one was open for 1% of the time, Pallas kernels for 0%

commit v1 on v0

v1 whole, which is shorter than its diff:
```python
import math

import jax
import jax.numpy as jnp
from jax import lax
from jax.experimental import pallas as pl
from jax.experimental.pallas import tpu as pltpu
from jax.sharding import PartitionSpec as P

MESH = pl.DeviceIdType.MESH
BF16, F32 = jnp.bfloat16, jnp.float32

LEARN, ROLL, NZ, NX, NH = 32, 16, 8, 4, 4
RANK, TOKENS, OWN = 128, 20480, 4
ROWS, HID, OUT, WCOLS = 640, 1792, 512, 896
PART = ROWS // NX
TD, TU, TW = HID // 128, OUT // 128, WCOLS // 128
PD, PU, PW = 64, 16, 32

STEP = 20
adapter_scale = 2.0
learning_rate = 0.001
beta_one = 0.9
beta_two = 0.999
epsilon = 1e-08
weight_decay = 0.01


def adam(weights, moment_one, moment_two, gradient):
    one_next = beta_one * moment_one + (1.0 - beta_one) * gradient
    two_next = beta_two * moment_two + (1.0 - beta_two) * gradient * gradient
    corr_one = 1.0 - beta_one**STEP
    corr_two = 1.0 - beta_two**STEP
    update = one_next / corr_one / (jnp.sqrt(two_next / corr_two) + epsilon)
    return weights - learning_rate * (update + weight_decay * weights), one_next, two_next


def onehot(rows, cols, column_of_row):
    row = lax.broadcasted_iota(jnp.int32, (rows, cols), 0)
    col = lax.broadcasted_iota(jnp.int32, (rows, cols), 1)
    return jnp.where(column_of_row(row) == col, 1.0, 0.0).astype(BF16)


def dot(a, b, ca, cb):
    return lax.dot_general(a, b, (((ca,), (cb,)), ((), ())), preferred_element_type=F32)


def pack(value, tiles, rows):
    parts = [value[:, 128 * t : 128 * t + 128] for t in range(tiles)]
    if rows > OWN * tiles:
        parts.append(jnp.zeros((rows - OWN * tiles, 128), value.dtype))
    return jnp.concatenate(parts, axis=0).astype(BF16)


def unpack(value, tiles):
    return jnp.concatenate([value[OWN * t : OWN * t + OWN] for t in range(tiles)], axis=1)


def kernel(
    w_hbm, x_hbm, g_hbm, dp_hbm, dm_hbm, dv_hbm, up_hbm, um_hbm, uv_hbm,
    wo_hbm, dpo_hbm, dmo_hbm, dvo_hbm, upo_hbm, umo_hbm, uvo_hbm,
    w_v, x_v, g_v, dp_v, dm_v, dv_v, up_v, um_v, uv_v,
    wo_v, dpo_v, dmo_v, dvo_v, upo_v, umo_v, uvo_v,
    ubuf, dbuf, umat, dmat, pu, pd, pdt, put, pw,
    bpart, bx, bh, blow, hpart, hx, hh, hlow,
    gpack, gcore, gsum, gz, upack, ured, unew, fsend, fbuf, dnew,
    load_sem, store_sem, send_sem, recv_sem,
):
    l = lax.axis_index("learn")
    r = lax.axis_index("roll")
    z, zy, q, core = l // 4, l // 2, l % 4, l % 2
    yhi, x = r // 4, r % 4
    core_peer = (l + 1 - 2 * core, r)
    ylo_peer = (l + 2 - 4 * (q // 2), r)

    loads = []
    for k, (src, dst) in enumerate(
        [(up_hbm, up_v), (dp_hbm, dp_v), (g_hbm, g_v), (x_hbm, x_v), (dm_hbm, dm_v), (dv_hbm, dv_v),
         (um_hbm, um_v), (uv_hbm, uv_v), (w_hbm, w_v)]
    ):
        copy = pltpu.make_async_copy(src, dst, load_sem.at[k])
        copy.start()
        loads.append(copy)
    load_up, load_dp, load_g, load_x, load_dm, load_dv, load_um, load_uv, load_w = loads

    barrier = pltpu.get_barrier_semaphore()

    def greet(to):
        pl.semaphore_signal(barrier, inc=1, device_id=to, device_id_type=MESH)

    for k in range(1, LEARN):
        greet(((l + k) % LEARN, r))
    for k in range(1, 4):
        greet((l, yhi * 4 + (x + k) % 4))
        greet((l, ((yhi + k) % 4) * 4 + x))
    source_roll = l // 2
    for k in range(1, LEARN):
        greet(((l + k) % LEARN, source_roll))
    at_home = r == source_roll

    greet((l, source_roll))

    load_up.wait()
    load_dp.wait()
    ubuf[l] = pack(up_v[...], TU, PU)
    dbuf[q, z] = pack(dp_v[...], TD, PD)
    pl.semaphore_wait(barrier, LEARN - 1 + 6 + LEARN)

    def rcopy(src, dst, k, to):
        return pltpu.make_async_remote_copy(
            src_ref=src, dst_ref=dst, send_sem=send_sem.at[k], recv_sem=recv_sem.at[k],
            device_id=to, device_id_type=MESH,
        )

    def drain(ref, sem):
        pltpu.make_async_copy(ref, ref, sem).wait()

    def learn_all(src_of, dst, k):
        def send(j, c):
            to = (l + j) % LEARN
            rcopy(src_of(to), dst.at[l], k, (to, r)).start()
            return c

        lax.fori_loop(1, LEARN, send, 0)

    def x_to(j):
        return yhi * 4 + (x + j) % 4

    def h_to(j):
        return ((yhi + j) % 4) * 4 + x

    learn_all(lambda to: ubuf.at[l], ubuf, 0)
    for j in range(1, NZ):
        rcopy(dbuf.at[q, z], dbuf.at[q, z], 1, (((z + j) % NZ) * 4 + q, r)).start()

    pu[...] = onehot(512, 512, lambda a: ((a & 127) >> 2) * 16 + (a >> 7) * 4 + (a & 3))
    pd[...] = onehot(448, 512, lambda a: ((a & 31) >> 2) * 64 + (a >> 5) * 4 + (a & 3))
    pdt[...] = onehot(
        512, 448,
        lambda a: jnp.where(
            (a & 63) < 56,
            ((a & 63) >> 2) * 32 + ((a >> 6) & 3) * 8 + (a >> 8) * 4 + (a & 3),
            -1,
        ),
    )
    put[...] = onehot(
        512, 512,
        lambda a: ((a & 15) >> 2) * 128 + ((a >> 4) & 3) * 32 + (a >> 6) * 4 + (a & 3),
    )
    pw[...] = onehot(448, 512, lambda a: ((a & 63) >> 2) * 32 + (a >> 6) * 4 + (a & 3))

    drain(ubuf.at[pl.ds(0, LEARN - 1)], recv_sem.at[0])
    spread = dot(pu[...], ubuf[...].reshape(512, 128), 1, 0).astype(BF16)
    for t in range(TU):
        umat[:, 128 * t : 128 * t + 128] = spread[128 * t : 128 * t + 128]
    load_g.wait()
    bpart[...] = dot(g_v[...], umat[...], 1, 1).astype(BF16).reshape(NX, PART, 128)
    for j in range(1, 4):
        rcopy(bpart.at[(x + j) % 4], bx.at[x], 2, (l, x_to(j))).start()
    bx[x] = bpart[x]

    drain(dbuf.at[0, pl.ds(0, NZ - 1)], recv_sem.at[1])
    rcopy(dbuf.at[q], dbuf.at[q], 3, core_peer).start()
    rcopy(dbuf.at[q], dbuf.at[q], 4, ylo_peer).start()

    def sum_four(buf):
        v = buf[...].astype(F32)
        return (v[0] + v[1]) + (v[2] + v[3])

    drain(bx.at[pl.ds(0, 3)], recv_sem.at[2])
    bh[yhi] = sum_four(bx).astype(BF16)
    for j in range(1, 4):
        rcopy(bh.at[yhi], bh.at[yhi], 5, (l, h_to(j))).start()

    drain(dbuf.at[0], recv_sem.at[4])
    q_other = (q + 2) % 4
    rcopy(dbuf.at[q_other], dbuf.at[q_other], 6, core_peer).start()
    drain(dbuf.at[0], recv_sem.at[3])
    drain(dbuf.at[0], recv_sem.at[6])
    for k in range(4):
        spread = dot(pd[...], dbuf[k].reshape(512, 128), 1, 0).astype(BF16)
        for t in range(TD):
            dmat[32 * k : 32 * k + 32, 128 * t : 128 * t + 128] = spread[32 * t : 32 * t + 32]
    load_x.wait()
    hpart[...] = dot(x_v[...], dmat[...], 1, 1).astype(BF16).reshape(NX, PART, 128)
    for j in range(1, 4):
        rcopy(hpart.at[(x + j) % 4], hx.at[x], 7, (l, x_to(j))).start()
    hx[x] = hpart[x]

    drain(bh.at[pl.ds(0, 3)], recv_sem.at[5])
    blow[x] = (adapter_scale * sum_four(bh)).astype(BF16)
    for j in range(1, 4):
        rcopy(blow.at[x], blow.at[x], 8, (l, x_to(j))).start()

    drain(hx.at[pl.ds(0, 3)], recv_sem.at[7])
    hh[yhi] = sum_four(hx).astype(BF16)
    for j in range(1, 4):
        rcopy(hh.at[yhi], hh.at[yhi], 9, (l, h_to(j))).start()

    normalizer_scale = 1.0 / math.sqrt(TOKENS)
    drain(blow.at[pl.ds(0, 3)], recv_sem.at[8])
    grad = (normalizer_scale * dot(blow[...].reshape(ROWS, 128), x_v[...], 0, 0)).astype(BF16)
    for k in range(4):
        stack = jnp.concatenate(
            [grad[32 * k : 32 * k + 32, 128 * t : 128 * t + 128] for t in range(TD)], axis=0
        )
        packed = dot(pdt[...], stack, 1, 0).astype(BF16)
        gpack[0, 4 * k : 4 * k + 4] = packed[:256].reshape(4, PD, 128)
        gpack[1, 4 * k : 4 * k + 4] = packed[256:].reshape(4, PD, 128)
    rcopy(gpack.at[1 - core], gcore, 10, core_peer).start()

    drain(hh.at[pl.ds(0, 3)], recv_sem.at[9])
    hlow[x] = sum_four(hh).astype(BF16)
    for j in range(1, 4):
        rcopy(hlow.at[x], hlow.at[x], 11, (l, x_to(j))).start()

    drain(gcore, recv_sem.at[10])
    gsum[...] = (gpack[core].astype(F32) + gcore[...].astype(F32)).astype(BF16)

    def send_gsum(j, c):
        to = (zy + j) % 16
        rcopy(gsum.at[to], gz.at[zy], 12, (to * 2 + core, r)).start()
        return c

    lax.fori_loop(1, 16, send_gsum, 0)
    gz[zy] = gsum[zy]

    drain(hlow.at[pl.ds(0, 3)], recv_sem.at[11])
    gradu = (adapter_scale * normalizer_scale) * dot(hlow[...].reshape(ROWS, 128), g_v[...], 0, 0)
    gradu = gradu.astype(BF16)
    stack = jnp.concatenate([gradu[:, 128 * t : 128 * t + 128] for t in range(TU)], axis=0)
    upack[...] = dot(put[...], stack, 1, 0).astype(BF16).reshape(LEARN, PU, 128)
    learn_all(lambda to: upack.at[to], ured, 13)
    ured[l] = upack[l]

    stores = []

    def store(k, src, dst):
        copy = pltpu.make_async_copy(src, dst, store_sem.at[k])
        copy.start()
        stores.append(copy)

    for copy in (load_dm, load_dv, load_um, load_uv, load_w):
        copy.wait()
    drain(gz.at[pl.ds(0, 15)], recv_sem.at[12])
    new_p, new_m, new_v = adam(
        dp_v[...], dm_v[...], dv_v[...], unpack(jnp.sum(gz[...].astype(F32), axis=0), TD)
    )
    fsend[0] = pack(new_p[:, :WCOLS], TW, PW)
    fsend[1] = pack(new_p[:, WCOLS:], TW, PW)

    def to_shard(k):
        return 2 * r + k // 16, k % 16

    def send_shard(k, c):
        to_l, to_r = to_shard(k)
        own = jnp.logical_and(to_l == l, to_r == r)

        @pl.when(jnp.logical_not(own))
        def _():
            rcopy(fsend.at[k // 16], fbuf.at[l], 14, (to_l, to_r)).start()

        @pl.when(own)
        def _():
            pltpu.make_async_copy(fsend.at[k // 16], fbuf.at[l], recv_sem.at[14]).start()

        return c

    lax.fori_loop(0, 32, send_shard, 0)
    dpo_v[...] = new_p
    dmo_v[...] = new_m
    dvo_v[...] = new_v
    store(0, dpo_v, dpo_hbm)
    store(1, dmo_v, dmo_hbm)
    store(2, dvo_v, dvo_hbm)

    drain(ured.at[pl.ds(0, LEARN - 1)], recv_sem.at[13])
    new_p, new_m, new_v = adam(
        up_v[...], um_v[...], uv_v[...], unpack(jnp.sum(ured[...].astype(F32), axis=0), TU)
    )
    unew[l] = pack(new_p, TU, PU)
    learn_all(lambda to: unew.at[l], unew, 15)
    upo_v[...] = new_p
    umo_v[...] = new_m
    uvo_v[...] = new_v
    store(3, upo_v, upo_hbm)
    store(4, umo_v, umo_hbm)
    store(5, uvo_v, uvo_hbm)

    drain(fbuf, recv_sem.at[14])
    for k in range(2):
        spread = dot(pw[...], fbuf[16 * k : 16 * k + 16].reshape(512, 128), 1, 0).astype(BF16)
        for t in range(TW):
            dnew[64 * k : 64 * k + 64, 128 * t : 128 * t + 128] = spread[64 * t : 64 * t + 64]
    drain(unew.at[pl.ds(0, LEARN - 1)], recv_sem.at[15])
    spread = dot(pu[...], unew[...].reshape(512, 128), 1, 0).astype(BF16)
    for t in range(TU):
        umat[:, 128 * t : 128 * t + 128] = spread[128 * t : 128 * t + 128]
    product = dot(umat[...], dnew[...], 0, 0)
    wo_v[...] = (w_v[...].astype(F32) + adapter_scale * product).astype(BF16)
    store(6, wo_v, wo_hbm)

    drain(ubuf.at[pl.ds(0, LEARN - 1)], send_sem.at[0])
    drain(dbuf.at[0, pl.ds(0, NZ - 1)], send_sem.at[1])
    for k in (3, 4, 6):
        drain(dbuf.at[0], send_sem.at[k])
    for k in (2, 5, 7, 8, 9, 11):
        drain(bx.at[pl.ds(0, 3)], send_sem.at[k])
    drain(gcore, send_sem.at[10])
    drain(gz.at[pl.ds(0, 15)], send_sem.at[12])
    drain(ured.at[pl.ds(0, LEARN - 1)], send_sem.at[13])
    drain(fbuf.at[pl.ds(0, LEARN - 1)], send_sem.at[14])

    @pl.when(jnp.logical_not(at_home))
    def _():
        drain(fbuf.at[0], send_sem.at[14])

    drain(unew.at[pl.ds(0, LEARN - 1)], send_sem.at[15])
    for copy in stores:
        copy.wait()


def per_device(*args):
    down, up = (OWN, HID), (OWN, OUT)
    small = [down, down, down, up, up, up]
    any_spec = pl.BlockSpec(memory_space=pl.ANY)

    def b(*shape):
        return pltpu.VMEM(shape, BF16)

    low = [b(NX, PART, 128) for _ in range(4)]
    return tuple(pl.pallas_call(
        kernel,
        out_shape=[jax.ShapeDtypeStruct((OUT, WCOLS), BF16)]
        + [jax.ShapeDtypeStruct(s, F32) for s in small],
        in_specs=[any_spec] * 9,
        out_specs=[any_spec] * 7,
        scratch_shapes=[b(OUT, WCOLS), b(ROWS, HID), b(ROWS, OUT)]
        + [pltpu.VMEM(s, F32) for s in small]
        + [b(OUT, WCOLS)]
        + [pltpu.VMEM(s, F32) for s in small]
        + [b(LEARN, PU, 128), b(4, NZ, PD, 128), b(RANK, OUT), b(RANK, HID)]
        + [b(512, 512), b(448, 512), b(512, 448), b(512, 512), b(448, 512)]
        + low
        + low
        + [b(2, 16, PD, 128), b(16, PD, 128), b(16, PD, 128), b(16, PD, 128)]
        + [b(LEARN, PU, 128), b(LEARN, PU, 128), b(LEARN, PU, 128)]
        + [b(2, PW, 128), b(LEARN, PW, 128), b(RANK, WCOLS)]
        + [pltpu.SemaphoreType.DMA((9,)), pltpu.SemaphoreType.DMA((7,))]
        + [pltpu.SemaphoreType.DMA((16,)), pltpu.SemaphoreType.DMA((16,))],
        compiler_params=pltpu.CompilerParams(
            collective_id=0, has_side_effects=True, vmem_limit_bytes=60 * 2**20
        ),
        cost_estimate=pl.CostEstimate(
            flops=10**9, bytes_accessed=6 * 10**6, transcendentals=0
        ),
        name="adapter_step",
    )(*args))


def solution(mesh):
    return jax.shard_map(
        per_device,
        mesh=mesh,
        in_specs=(P("roll", "learn"),) + (P("learn", "roll"),) * 8,
        out_specs=(P("roll", "learn"),) + (P("learn", "roll"),) * 6,
        check_vma=False,
    )
```

time: 596 us -> 101 us (0.17)
  waiting for transfers between devices: 345 us -> 0 us
  blocking collectives: 216 us -> 0 us
  Pallas kernels: 0 us -> 89.5 us
  between operations: 13.9 us -> 0.65 us
  matrix products: 8.46 us -> 0 us
  local copies, waits for them, and re-layouts: 1.87 us -> 10.1 us
    psum x2 -> x0, waiting for transfers between devices: 273 us -> none  [the longest x1 230 us: per_device(): lax.psum(jnp.concatenate([left_part, right_operand], axis=1).astype(jnp.b...]
    all_gather x4 -> x0, blocking collectives: 144 us -> none  [the longest x1 42.2 us: per_device(): lax.all_gather(adapter_up_factor.astype(jnp.bfloat16), 'learn', axis=0, t...]
    pallas_call x0 -> x1, Pallas kernels: none -> 89.5 us  [per_device(): pl.pallas_call(kernel, out_shape=[jax.ShapeDtypeStruct((OUT, WCOLS), BF16...]
    psum x1 -> x0, blocking collectives: 72.3 us -> none  [per_device(): hidden_sum, backward_total = lax.psum((hidden_part, back_part), 'roll')]
    all_gather x1 -> x0, waiting for transfers between devices: 72 us -> none  [per_device(): every_column = lax.all_gather(rank_rows, 'roll', axis=1, tiled=True)]
    dot_general x5 -> x0, matrix products: 8.46 us -> none  [the longest x3 4.48 us: contraction_rows(): lax.dot_general(left, right, (((0,), (0,)), ((), ())), preferred_element_...]
    unnamed x20 -> x7, local copies, waits for them, and re-layouts: 1.87 us -> 10.1 us
  transfers between devices with their start and end apart: 3 -> 0, of which waited for: 3 -> 0; matrix products, arithmetic and copies ran while one was open for 1% -> 0% of each run, Pallas kernels for 0% -> 0%
where the time goes in v1:
time: 101 us; the launch traced here: 100 us
  Pallas kernels  89.5 us (89%)
  local copies, waits for them, and re-layouts  10.1 us (10%)
    pallas_call x1, Pallas kernels, per_device(): pl.pallas_call(kernel, out_shape=[jax.ShapeDtypeStruct((OUT, WCOLS), BF16...  89.5 us
    unnamed x7, local copies, waits for them, and re-layouts  10.1 us

profile of v1, /device:TPU:1, one launch (start us, length us, event | category | flops | bytes accessed | tf_op | source)
XLA Modules:
  0.0 100.3 jit_solution(10397149835815278984)
XLA Ops:
  0.6 89.5 %adapter_step.1 = (bf16[512,896]{1,0:T(8,128)(2,1)}, f32[4,1792]{1,0:T(4,128)}, f32[4,1792]{1,0:T(4,128)}, f32[4,1792]{1,0:T(4,128)}, f32[4,512]{1,0:T(4,128)}, /*index=5*/f32[4,512]{1,0:T(4,128)}, f32[4,512]{1,0:T(4,128)}) custom-call(bf16[512,896]{1,0:T(8,128)(2,1)} %w_hbm.1, bf16[640,1792]{1,0:T(8,128)(2,1)} %x_hbm.1, bf16[640,512]{1,0:T(8,128)(2,1)} %g_hbm.1, ...), custom_call_target="tpu_custom_call" | custom-call | flops 1000000000 | bytes 6000000 | tf_op jit(solution)/shard_map/adapter_step/pallas_call | solution.py:332
  90.1 2.2 %copy.23 = bf16[512,896]{1,0:T(8,128)(2,1)} copy(bf16[512,896]{1,0:T(8,128)(2,1)} %get-tuple-element.14) | data formatting | bytes 1835008
  92.3 1.4 %copy.24 = f32[4,1792]{1,0:T(4,128)} copy(f32[4,1792]{1,0:T(4,128)} %get-tuple-element.15) | data formatting | bytes 57344
  93.7 1.4 %copy.25 = f32[4,1792]{1,0:T(4,128)} copy(f32[4,1792]{1,0:T(4,128)} %get-tuple-element.16) | data formatting | bytes 57344
  95.0 1.4 %copy.26 = f32[4,1792]{1,0:T(4,128)} copy(f32[4,1792]{1,0:T(4,128)} %get-tuple-element.17) | data formatting | bytes 57344
  96.4 1.3 %copy.27 = f32[4,512]{1,0:T(4,128)} copy(f32[4,512]{1,0:T(4,128)} %get-tuple-element.18) | data formatting | bytes 16384
  97.7 1.3 %copy.28 = f32[4,512]{1,0:T(4,128)} copy(f32[4,512]{1,0:T(4,128)} %get-tuple-element.19) | data formatting | bytes 16384
  99.0 1.3 %copy.29 = f32[4,512]{1,0:T(4,128)} copy(f32[4,512]{1,0:T(4,128)} %get-tuple-element.20) | data formatting | bytes 16384

commit v2 on v1

v2 whole, which is shorter than its diff:
```python
import math

import jax
import jax.numpy as jnp
from jax import lax
from jax.experimental import pallas as pl
from jax.experimental.pallas import tpu as pltpu
from jax.sharding import PartitionSpec as P

MESH = pl.DeviceIdType.MESH
BF16, F32 = jnp.bfloat16, jnp.float32

LEARN, ROLL, NZ, NX, NH = 32, 16, 8, 4, 4
RANK, TOKENS, OWN = 128, 20480, 4
ROWS, HID, OUT, WCOLS = 640, 1792, 512, 896
PART = ROWS // NX
TD, TU, TW = HID // 128, OUT // 128, WCOLS // 128
PD, PU, PW = 64, 16, 32

STEP = 20
adapter_scale = 2.0
learning_rate = 0.001
beta_one = 0.9
beta_two = 0.999
epsilon = 1e-08
weight_decay = 0.01


def adam(weights, moment_one, moment_two, gradient):
    one_next = beta_one * moment_one + (1.0 - beta_one) * gradient
    two_next = beta_two * moment_two + (1.0 - beta_two) * gradient * gradient
    corr_one = 1.0 - beta_one**STEP
    corr_two = 1.0 - beta_two**STEP
    update = one_next / corr_one / (jnp.sqrt(two_next / corr_two) + epsilon)
    return weights - learning_rate * (update + weight_decay * weights), one_next, two_next


def onehot(rows, cols, column_of_row):
    row = lax.broadcasted_iota(jnp.int32, (rows, cols), 0)
    col = lax.broadcasted_iota(jnp.int32, (rows, cols), 1)
    return jnp.where(column_of_row(row) == col, 1.0, 0.0).astype(BF16)


def dot(a, b, ca, cb):
    return lax.dot_general(a, b, (((ca,), (cb,)), ((), ())), preferred_element_type=F32)


def pack(value, tiles, rows):
    parts = [value[:, 128 * t : 128 * t + 128] for t in range(tiles)]
    if rows > OWN * tiles:
        parts.append(jnp.zeros((rows - OWN * tiles, 128), value.dtype))
    return jnp.concatenate(parts, axis=0).astype(BF16)


def unpack(value, tiles):
    return jnp.concatenate([value[OWN * t : OWN * t + OWN] for t in range(tiles)], axis=1)


def kernel(
    w_hbm, x_hbm, g_hbm, dp_hbm, dm_hbm, dv_hbm, up_hbm, um_hbm, uv_hbm,
    w_v, umat, dnew, dpo, dmo, dvo, upo, umo, uvo,
    x_v, g_v, dp_v, dm_v, dv_v, up_v, um_v, uv_v,
    ubuf, dbuf, dmat, pu, pd, pdt, put, pw,
    bpart, bx, bh, blow, hpart, hx, hh, hlow,
    gpack, gcore, gsum, gz, upack, ured, unew, fsend, fbuf,
    load_sem, send_sem, recv_sem,
):
    l = lax.axis_index("learn")
    r = lax.axis_index("roll")
    z, zy, q, core = l // 4, l // 2, l % 4, l % 2
    yhi, x = r // 4, r % 4
    core_peer = (l + 1 - 2 * core, r)
    ylo_peer = (l + 2 - 4 * (q // 2), r)
    source_roll = l // 2
    at_home = r == source_roll

    barrier = pltpu.get_barrier_semaphore()

    def greet(to):
        pl.semaphore_signal(barrier, inc=1, device_id=to, device_id_type=MESH)

    for k in range(1, LEARN):
        greet(((l + k) % LEARN, r))
    for k in range(1, 4):
        greet((l, yhi * 4 + (x + k) % 4))
        greet((l, ((yhi + k) % 4) * 4 + x))
    for k in range(LEARN):
        greet(((l + k) % LEARN, source_roll))

    loads = []
    for k, (src, dst) in enumerate(
        [(up_hbm, up_v), (dp_hbm, dp_v), (g_hbm, g_v), (x_hbm, x_v), (dm_hbm, dm_v), (dv_hbm, dv_v),
         (um_hbm, um_v), (uv_hbm, uv_v), (w_hbm, w_v)]
    ):
        copy = pltpu.make_async_copy(src, dst, load_sem.at[k])
        copy.start()
        loads.append(copy)
    load_up, load_dp, load_g, load_x = loads[:4]

    load_up.wait()
    load_dp.wait()
    ubuf[l] = pack(up_v[...], TU, PU)
    dbuf[q, z] = pack(dp_v[...], TD, PD)
    pl.semaphore_wait(barrier, LEARN - 1 + 6 + LEARN)

    arriving, leaving = {}, []

    def rcopy(src, dst, k, to):
        return pltpu.make_async_remote_copy(
            src_ref=src, dst_ref=dst, send_sem=send_sem.at[k], recv_sem=recv_sem.at[k],
            device_id=to, device_id_type=MESH,
        )

    def drain(ref, sem):
        pltpu.make_async_copy(ref, ref, sem).wait()

    def sent(k, ref):
        arriving[k] = ref
        leaving.append((k, ref))

    def receive(k):
        drain(arriving.pop(k), recv_sem.at[k])

    def finish():
        for k in list(arriving):
            receive(k)
        for k, ref in leaving:
            if k != 14:
                drain(ref, send_sem.at[k])
        if any(k == 14 for k, _ in leaving):
            drain(fbuf.at[pl.ds(0, LEARN - 1)], send_sem.at[14])

            @pl.when(jnp.logical_not(at_home))
            def _():
                drain(fbuf.at[0], send_sem.at[14])

    def learn_all(src_of, dst, k):
        def send(j, c):
            to = (l + j) % LEARN
            rcopy(src_of(to), dst.at[l], k, (to, r)).start()
            return c

        lax.fori_loop(1, LEARN, send, 0)
        sent(k, dst.at[pl.ds(0, LEARN - 1)])

    def x_to(j):
        return yhi * 4 + (x + j) % 4

    def h_to(j):
        return ((yhi + j) % 4) * 4 + x

    learn_all(lambda to: ubuf.at[l], ubuf, 0)
    for j in range(1, NZ):
        rcopy(dbuf.at[q, z], dbuf.at[q, z], 1, (((z + j) % NZ) * 4 + q, r)).start()
    sent(1, dbuf.at[0, pl.ds(0, NZ - 1)])

    pu[...] = onehot(512, 512, lambda a: ((a & 127) >> 2) * 16 + (a >> 7) * 4 + (a & 3))
    pd[...] = onehot(448, 512, lambda a: ((a & 31) >> 2) * 64 + (a >> 5) * 4 + (a & 3))
    pdt[...] = onehot(
        512, 448,
        lambda a: jnp.where(
            (a & 63) < 56,
            ((a & 63) >> 2) * 32 + ((a >> 6) & 3) * 8 + (a >> 8) * 4 + (a & 3),
            -1,
        ),
    )
    put[...] = onehot(
        512, 512,
        lambda a: ((a & 15) >> 2) * 128 + ((a >> 4) & 3) * 32 + (a >> 6) * 4 + (a & 3),
    )

    pw[...] = onehot(448, 512, lambda a: ((a & 63) >> 2) * 32 + (a >> 6) * 4 + (a & 3))

    receive(0)
    spread = dot(pu[...], ubuf[...].reshape(512, 128), 1, 0).astype(BF16)
    for t in range(TU):
        umat[:, 128 * t : 128 * t + 128] = spread[128 * t : 128 * t + 128]
    load_g.wait()
    bpart[...] = dot(g_v[...], umat[...], 1, 1).astype(BF16).reshape(NX, PART, 128)
    for j in range(1, 4):
        rcopy(bpart.at[(x + j) % 4], bx.at[x], 2, (l, x_to(j))).start()
    sent(2, bx.at[pl.ds(0, 3)])
    bx[x] = bpart[x]

    receive(1)
    rcopy(dbuf.at[q], dbuf.at[q], 3, core_peer).start()
    sent(3, dbuf.at[0])
    rcopy(dbuf.at[q], dbuf.at[q], 4, ylo_peer).start()
    sent(4, dbuf.at[0])

    def sum_four(buf):
        v = buf[...].astype(F32)
        return (v[0] + v[1]) + (v[2] + v[3])

    receive(2)
    bh[yhi] = sum_four(bx).astype(BF16)
    for j in range(1, 4):
        rcopy(bh.at[yhi], bh.at[yhi], 5, (l, h_to(j))).start()
    sent(5, bh.at[pl.ds(0, 3)])

    receive(4)
    q_other = (q + 2) % 4
    rcopy(dbuf.at[q_other], dbuf.at[q_other], 6, core_peer).start()
    sent(6, dbuf.at[0])
    receive(3)
    receive(6)
    for k in range(4):
        spread = dot(pd[...], dbuf[k].reshape(512, 128), 1, 0).astype(BF16)
        for t in range(TD):
            dmat[32 * k : 32 * k + 32, 128 * t : 128 * t + 128] = spread[32 * t : 32 * t + 32]
    load_x.wait()
    hpart[...] = dot(x_v[...], dmat[...], 1, 1).astype(BF16).reshape(NX, PART, 128)
    for j in range(1, 4):
        rcopy(hpart.at[(x + j) % 4], hx.at[x], 7, (l, x_to(j))).start()
    sent(7, hx.at[pl.ds(0, 3)])
    hx[x] = hpart[x]

    receive(5)
    blow[x] = (adapter_scale * sum_four(bh)).astype(BF16)
    for j in range(1, 4):
        rcopy(blow.at[x], blow.at[x], 8, (l, x_to(j))).start()
    sent(8, blow.at[pl.ds(0, 3)])

    receive(7)
    hh[yhi] = sum_four(hx).astype(BF16)
    for j in range(1, 4):
        rcopy(hh.at[yhi], hh.at[yhi], 9, (l, h_to(j))).start()
    sent(9, hh.at[pl.ds(0, 3)])

    normalizer_scale = 1.0 / math.sqrt(TOKENS)
    receive(8)
    grad = (normalizer_scale * dot(blow[...].reshape(ROWS, 128), x_v[...], 0, 0)).astype(BF16)
    for k in range(4):
        stack = jnp.concatenate(
            [grad[32 * k : 32 * k + 32, 128 * t : 128 * t + 128] for t in range(TD)], axis=0
        )
        packed = dot(pdt[...], stack, 1, 0).astype(BF16)
        gpack[0, 4 * k : 4 * k + 4] = packed[:256].reshape(4, PD, 128)
        gpack[1, 4 * k : 4 * k + 4] = packed[256:].reshape(4, PD, 128)
    rcopy(gpack.at[1 - core], gcore, 10, core_peer).start()
    sent(10, gcore)

    receive(9)
    hlow[x] = sum_four(hh).astype(BF16)
    for j in range(1, 4):
        rcopy(hlow.at[x], hlow.at[x], 11, (l, x_to(j))).start()
    sent(11, hlow.at[pl.ds(0, 3)])

    receive(10)
    gsum[...] = (gpack[core].astype(F32) + gcore[...].astype(F32)).astype(BF16)

    def send_gsum(j, c):
        to = (zy + j) % 16
        rcopy(gsum.at[to], gz.at[zy], 12, (to * 2 + core, r)).start()
        return c

    lax.fori_loop(1, 16, send_gsum, 0)
    sent(12, gz.at[pl.ds(0, 15)])
    gz[zy] = gsum[zy]

    receive(11)
    gradu = (adapter_scale * normalizer_scale) * dot(hlow[...].reshape(ROWS, 128), g_v[...], 0, 0)
    gradu = gradu.astype(BF16)
    stack = jnp.concatenate([gradu[:, 128 * t : 128 * t + 128] for t in range(TU)], axis=0)
    upack[...] = dot(put[...], stack, 1, 0).astype(BF16).reshape(LEARN, PU, 128)
    learn_all(lambda to: upack.at[to], ured, 13)
    ured[l] = upack[l]

    for copy in loads[4:]:
        copy.wait()
    receive(12)
    gradient = unpack(jnp.sum(gz[...].astype(F32), axis=0), TD)
    new_p, new_m, new_v = adam(dp_v[...], dm_v[...], dv_v[...], gradient)
    fsend[0] = pack(new_p[:, :WCOLS], TW, PW)
    fsend[1] = pack(new_p[:, WCOLS:], TW, PW)

    def send_shard(k, c):
        to_l, to_r = 2 * r + k // 16, k % 16
        own = jnp.logical_and(to_l == l, to_r == r)

        @pl.when(jnp.logical_not(own))
        def _():
            rcopy(fsend.at[k // 16], fbuf.at[l], 14, (to_l, to_r)).start()

        @pl.when(own)
        def _():
            pltpu.make_async_copy(fsend.at[k // 16], fbuf.at[l], recv_sem.at[14]).start()

        return c

    lax.fori_loop(0, 32, send_shard, 0)
    sent(14, fbuf)
    dpo[...] = new_p
    dmo[...] = new_m
    dvo[...] = new_v

    receive(13)
    gradient = unpack(jnp.sum(ured[...].astype(F32), axis=0), TU)
    new_p, new_m, new_v = adam(up_v[...], um_v[...], uv_v[...], gradient)
    unew[l] = pack(new_p, TU, PU)
    learn_all(lambda to: unew.at[l], unew, 15)

    upo[...] = new_p
    umo[...] = new_m
    uvo[...] = new_v

    receive(14)
    for k in range(2):
        spread = dot(pw[...], fbuf[16 * k : 16 * k + 16].reshape(512, 128), 1, 0).astype(BF16)
        for t in range(TW):
            dnew[64 * k : 64 * k + 64, 128 * t : 128 * t + 128] = spread[64 * t : 64 * t + 64]
    receive(15)
    spread = dot(pu[...], unew[...].reshape(512, 128), 1, 0).astype(BF16)
    for t in range(TU):
        umat[:, 128 * t : 128 * t + 128] = spread[128 * t : 128 * t + 128]
    finish()


def merge_kernel(w, umat, dnew, *refs):
    moved, wo_hbm, stored, wo_v, store_sem = refs[:6], refs[6], refs[7:13], refs[13], refs[14]
    stores = []

    def store(src, dst):
        copy = pltpu.make_async_copy(src, dst, store_sem.at[len(stores)])
        copy.start()
        stores.append(copy)

    for src, dst in zip(moved, stored):
        store(src, dst)
    for k in range(4):
        rows = slice(128 * k, 128 * k + 128)
        product = dot(umat[:, rows], dnew[...], 0, 0)
        wo_v[rows] = (w[rows].astype(F32) + adapter_scale * product).astype(BF16)
        store(wo_v.at[rows], wo_hbm.at[rows])
    for copy in stores:
        copy.wait()


def per_device(*args):
    down, up = (OWN, HID), (OWN, OUT)
    small = [down, down, down, up, up, up]
    hbm = pl.BlockSpec(memory_space=pltpu.HBM)
    vmem = pl.BlockSpec(memory_space=pltpu.VMEM)
    dma = pltpu.SemaphoreType.DMA

    def b(*shape):
        return pltpu.VMEM(shape, BF16)

    states = [jax.ShapeDtypeStruct(s, F32) for s in small]
    low = [b(NX, PART, 128) for _ in range(4)]
    made = pl.pallas_call(
        kernel,
        out_shape=[
            jax.ShapeDtypeStruct((OUT, WCOLS), BF16),
            jax.ShapeDtypeStruct((RANK, OUT), BF16),
            jax.ShapeDtypeStruct((RANK, WCOLS), BF16),
        ]
        + states,
        in_specs=[hbm] * 9,
        out_specs=[vmem] * 9,
        scratch_shapes=[b(ROWS, HID), b(ROWS, OUT)]
        + [pltpu.VMEM(s, F32) for s in small]
        + [b(LEARN, PU, 128), b(4, NZ, PD, 128), b(RANK, HID)]
        + [b(512, 512), b(448, 512), b(512, 448), b(512, 512), b(448, 512)]
        + low
        + low
        + [b(2, 16, PD, 128), b(16, PD, 128), b(16, PD, 128), b(16, PD, 128)]
        + [b(LEARN, PU, 128), b(LEARN, PU, 128), b(LEARN, PU, 128)]
        + [b(2, PW, 128), b(LEARN, PW, 128)]
        + [dma((9,)), dma((16,)), dma((16,))],
        compiler_params=pltpu.CompilerParams(
            collective_id=0, has_side_effects=True, vmem_limit_bytes=40 * 2**20
        ),
        cost_estimate=pl.CostEstimate(flops=10**9, bytes_accessed=10**7, transcendentals=0),
        name="adapter_step",
    )(*(pltpu.with_memory_space_constraint(a, pltpu.HBM) for a in args))
    return tuple(
        pl.pallas_call(
            merge_kernel,
            out_shape=[jax.ShapeDtypeStruct((OUT, WCOLS), BF16)] + states,
            in_specs=[vmem] * 9,
            out_specs=[hbm] * 7,
            scratch_shapes=[b(OUT, WCOLS), dma((10,))],
            compiler_params=pltpu.CompilerParams(vmem_limit_bytes=20 * 2**20),
            cost_estimate=pl.CostEstimate(flops=10**8, bytes_accessed=2 * 10**6, transcendentals=0),
            name="merge",
        )(*made)
    )


def solution(mesh):
    return jax.shard_map(
        per_device,
        mesh=mesh,
        in_specs=(P("roll", "learn"),) + (P("learn", "roll"),) * 8,
        out_specs=(P("roll", "learn"),) + (P("learn", "roll"),) * 6,
        check_vma=False,
    )
```

time: 101 us -> 88.7 us (0.88)
  local copies, waits for them, and re-layouts: 10.1 us -> 0 us
  Pallas kernels: 89.5 us -> 87.9 us
    unnamed x7 -> x0, local copies, waits for them, and re-layouts: 10.1 us -> none
    pallas_call x1, Pallas kernels: 89.5 us -> 86.7 us  [per_device(): pl.pallas_call(kernel, out_shape=[jax.ShapeDtypeStruct((OUT, WCOLS), BF16...]
    pallas_call x0 -> x1, Pallas kernels: none -> 1.27 us  [per_device(): pl.pallas_call(merge_kernel, out_shape=[jax.ShapeDtypeStruct((OUT, WCOLS)...]
where the time goes in v2:
time: 88.7 us; the launch traced here: 88.6 us
  Pallas kernels  87.9 us (99%)
    pallas_call x1, Pallas kernels, per_device(): pl.pallas_call(kernel, out_shape=[jax.ShapeDtypeStruct((OUT, WCOLS), BF16...  86.7 us

profile of v2, /device:TPU:1, one launch (start us, length us, event | category | flops | bytes accessed | tf_op | source)
XLA Modules:
  0.0 88.6 jit_solution(12533421062381635477)
XLA Ops:
  0.6 86.7 %adapter_step.1 = (bf16[512,896]{1,0:T(8,128)(2,1)S(1)}, bf16[128,512]{1,0:T(8,128)(2,1)S(1)}, bf16[128,896]{1,0:T(8,128)(2,1)S(1)}, f32[4,1792]{1,0:T(4,128)S(1...) custom-call(bf16[512,896]{1,0:T(8,128)(2,1)} %w_hbm.1, ...), custom_call_target="tpu_custom_call" | custom-call | flops 1000000000 | bytes 10000000 | tf_op jit(solution)/shard_map/adapter_step/pallas_call | solution.py:351
  87.3 1.3 %merge.1 = (bf16[512,896]{1,0:T(8,128)(2,1)}, f32[4,1792]{1,0:T(4,128)}, f32[4,1792]{1,0:T(4,128)}, f32[4,1792]{1,0:T(4,128)}, f32[4,512]{1,0:T(4,128)}, /*index=5*/f32[4,512]{1,0:T(4,128)}, f32[4,512]{1,0:T(4,128)}) custom-call(bf16[512,896]{1,0:T(8,128)(2,1)S(1)} %get-tuple-element.16.w, bf16[128,512]{1,0:T(8,128)(2,1)S(1)} %get-tuple-element.17.umat, ...), custom_call_target="tpu_custom_call" | custom-call | flops 100000000 | bytes 2000000 | tf_op jit(solution)/shard_map/merge/pallas_call | solution.py:378

commit v3 on v2

--- a/solution.py
+++ b/solution.py
@@ -10,7 +10,8 @@
 MESH = pl.DeviceIdType.MESH
 BF16, F32 = jnp.bfloat16, jnp.float32
 
-LEARN, ROLL, NZ, NX, NH = 32, 16, 8, 4, 4
+LEARN, ROLL, NX = 32, 16, 4
+FAR_FIRST = (10, 6, 14, 9, 11, 8, 5, 7, 13, 15, 4, 12, 2, 1, 3)
 RANK, TOKENS, OWN = 128, 20480, 4
 ROWS, HID, OUT, WCOLS = 640, 1792, 512, 896
 PART = ROWS // NX
@@ -62,17 +63,15 @@
     x_v, g_v, dp_v, dm_v, dv_v, up_v, um_v, uv_v,
     ubuf, dbuf, dmat, pu, pd, pdt, put, pw,
     bpart, bx, bh, blow, hpart, hx, hh, hlow,
-    gpack, gcore, gsum, gz, upack, ured, unew, fsend, fbuf,
-    load_sem, send_sem, recv_sem,
+    gpack, gcore, gsum, gz, upack, ured, unew, fgat, fbuf,
+    load_sem, send_sem, recv_sem, roll_sem,
 ):
     l = lax.axis_index("learn")
     r = lax.axis_index("roll")
-    z, zy, q, core = l // 4, l // 2, l % 4, l % 2
+    zy, core = l // 2, l % 2
     yhi, x = r // 4, r % 4
     core_peer = (l + 1 - 2 * core, r)
-    ylo_peer = (l + 2 - 4 * (q // 2), r)
-    source_roll = l // 2
-    at_home = r == source_roll
+    slot = core * 16 + zy
 
     barrier = pltpu.get_barrier_semaphore()
 
@@ -81,11 +80,8 @@
 
     for k in range(1, LEARN):
         greet(((l + k) % LEARN, r))
-    for k in range(1, 4):
-        greet((l, yhi * 4 + (x + k) % 4))
-        greet((l, ((yhi + k) % 4) * 4 + x))
-    for k in range(LEARN):
-        greet(((l + k) % LEARN, source_roll))
+    for k in range(1, ROLL):
+        greet((l, (r + k) % ROLL))
 
     loads = []
     for k, (src, dst) in enumerate(
@@ -99,15 +95,16 @@
 
     load_up.wait()
     load_dp.wait()
-    ubuf[l] = pack(up_v[...], TU, PU)
-    dbuf[q, z] = pack(dp_v[...], TD, PD)
-    pl.semaphore_wait(barrier, LEARN - 1 + 6 + LEARN)
+    ubuf[slot] = pack(up_v[...], TU, PU)
+    dbuf[slot] = pack(dp_v[...], TD, PD)
+    pl.semaphore_wait(barrier, LEARN + ROLL - 2)
 
     arriving, leaving = {}, []
 
-    def rcopy(src, dst, k, to):
+    def rcopy(src, dst, k, to, sem=None):
         return pltpu.make_async_remote_copy(
-            src_ref=src, dst_ref=dst, send_sem=send_sem.at[k], recv_sem=recv_sem.at[k],
+            src_ref=src, dst_ref=dst, send_sem=send_sem.at[k],
+            recv_sem=recv_sem.at[k] if sem is None else sem,
             device_id=to, device_id_type=MESH,
         )
 
@@ -125,23 +122,23 @@
         for k in list(arriving):
             receive(k)
         for k, ref in leaving:
-            if k != 14:
-                drain(ref, send_sem.at[k])
-        if any(k == 14 for k, _ in leaving):
-            drain(fbuf.at[pl.ds(0, LEARN - 1)], send_sem.at[14])
-
-            @pl.when(jnp.logical_not(at_home))
-            def _():
-                drain(fbuf.at[0], send_sem.at[14])
+            drain(ref, send_sem.at[k])
 
     def learn_all(src_of, dst, k):
         def send(j, c):
             to = (l + j) % LEARN
-            rcopy(src_of(to), dst.at[l], k, (to, r)).start()
+            rcopy(src_of(to), dst, k, (to, r)).start()
             return c
 
         lax.fori_loop(1, LEARN, send, 0)
-        sent(k, dst.at[pl.ds(0, LEARN - 1)])
+
+    def zy_all(src_of, dst, k):
+        def send(j, c):
+            to = (zy + j) % 16
+            rcopy(src_of(to), dst, k, (to * 2 + core, r)).start()
+            return c
+
+        lax.fori_loop(1, 16, send, 0)
 
     def x_to(j):
         return yhi * 4 + (x + j) % 4
@@ -149,12 +146,25 @@
     def h_to(j):
         return ((yhi + j) % 4) * 4 + x
 
-    learn_all(lambda to: ubuf.at[l], ubuf, 0)
-    for j in range(1, NZ):
-        rcopy(dbuf.at[q, z], dbuf.at[q, z], 1, (((z + j) % NZ) * 4 + q, r)).start()
-    sent(1, dbuf.at[0, pl.ds(0, NZ - 1)])
-
-    pu[...] = onehot(512, 512, lambda a: ((a & 127) >> 2) * 16 + (a >> 7) * 4 + (a & 3))
+    def x_all(src_of, dst, buf, k):
+        for j in (2, 1, 3):
+            rcopy(src_of((x + j) % 4), dst, k, (l, x_to(j))).start()
+        sent(k, buf.at[pl.ds(0, 3)])
+
+    def h_all(src, dst, buf, k):
+        for j in (2, 1, 3):
+            rcopy(src, dst, k, (l, h_to(j))).start()
+        sent(k, buf.at[pl.ds(0, 3)])
+
+    zy_all(lambda to: ubuf.at[slot], ubuf.at[slot], 0)
+    sent(0, ubuf.at[pl.ds(0, 15)])
+    zy_all(lambda to: dbuf.at[slot], dbuf.at[slot], 1)
+    sent(1, dbuf.at[pl.ds(0, 15)])
+    half = pl.ds(core * 16, 16)
+
+    pu[...] = onehot(
+        512, 512, lambda a: ((a >> 2) & 1) * 256 + ((a & 127) >> 3) * 16 + (a >> 7) * 4 + (a & 3)
+    )
     pd[...] = onehot(448, 512, lambda a: ((a & 31) >> 2) * 64 + (a >> 5) * 4 + (a & 3))
     pdt[...] = onehot(
         512, 448,
@@ -166,66 +176,51 @@
     )
     put[...] = onehot(
         512, 512,
-        lambda a: ((a & 15) >> 2) * 128 + ((a >> 4) & 3) * 32 + (a >> 6) * 4 + (a & 3),
-    )
-
+        lambda a: ((a & 15) >> 2) * 128 + ((a >> 4) & 1) * 64 + (a >> 5) * 4 + (a & 3),
+    )
     pw[...] = onehot(448, 512, lambda a: ((a & 63) >> 2) * 32 + (a >> 6) * 4 + (a & 3))
 
-    receive(0)
-    spread = dot(pu[...], ubuf[...].reshape(512, 128), 1, 0).astype(BF16)
-    for t in range(TU):
-        umat[:, 128 * t : 128 * t + 128] = spread[128 * t : 128 * t + 128]
-    load_g.wait()
-    bpart[...] = dot(g_v[...], umat[...], 1, 1).astype(BF16).reshape(NX, PART, 128)
-    for j in range(1, 4):
-        rcopy(bpart.at[(x + j) % 4], bx.at[x], 2, (l, x_to(j))).start()
-    sent(2, bx.at[pl.ds(0, 3)])
-    bx[x] = bpart[x]
-
-    receive(1)
-    rcopy(dbuf.at[q], dbuf.at[q], 3, core_peer).start()
-    sent(3, dbuf.at[0])
-    rcopy(dbuf.at[q], dbuf.at[q], 4, ylo_peer).start()
-    sent(4, dbuf.at[0])
+    def unpack_up(buf):
+        spread = dot(pu[...], buf[...].reshape(512, 128), 1, 0).astype(BF16)
+        for t in range(TU):
+            umat[:, 128 * t : 128 * t + 128] = spread[128 * t : 128 * t + 128]
 
     def sum_four(buf):
         v = buf[...].astype(F32)
         return (v[0] + v[1]) + (v[2] + v[3])
 
+    receive(0)
+    rcopy(ubuf.at[half], ubuf.at[half], 2, core_peer).start()
+    sent(2, ubuf.at[pl.ds(0, 16)])
+    load_g.wait()
     receive(2)
-    bh[yhi] = sum_four(bx).astype(BF16)
-    for j in range(1, 4):
-        rcopy(bh.at[yhi], bh.at[yhi], 5, (l, h_to(j))).start()
-    sent(5, bh.at[pl.ds(0, 3)])
-
+    unpack_up(ubuf)
+    bpart[...] = dot(g_v[...], umat[...], 1, 1).astype(BF16).reshape(NX, PART, 128)
+    x_all(lambda to: bpart.at[to], bx.at[x], bx, 3)
+    bx[x] = bpart[x]
+
+    receive(1)
+    rcopy(dbuf.at[half], dbuf.at[half], 4, core_peer).start()
+    sent(4, dbuf.at[pl.ds(0, 16)])
+    load_x.wait()
     receive(4)
-    q_other = (q + 2) % 4
-    rcopy(dbuf.at[q_other], dbuf.at[q_other], 6, core_peer).start()
-    sent(6, dbuf.at[0])
-    receive(3)
-    receive(6)
     for k in range(4):
-        spread = dot(pd[...], dbuf[k].reshape(512, 128), 1, 0).astype(BF16)
+        spread = dot(pd[...], dbuf[8 * k : 8 * k + 8].reshape(512, 128), 1, 0).astype(BF16)
         for t in range(TD):
             dmat[32 * k : 32 * k + 32, 128 * t : 128 * t + 128] = spread[32 * t : 32 * t + 32]
-    load_x.wait()
     hpart[...] = dot(x_v[...], dmat[...], 1, 1).astype(BF16).reshape(NX, PART, 128)
-    for j in range(1, 4):
-        rcopy(hpart.at[(x + j) % 4], hx.at[x], 7, (l, x_to(j))).start()
-    sent(7, hx.at[pl.ds(0, 3)])
+    x_all(lambda to: hpart.at[to], hx.at[x], hx, 5)
     hx[x] = hpart[x]
 
+    receive(3)
+    bh[yhi] = sum_four(bx).astype(BF16)
+    h_all(bh.at[yhi], bh.at[yhi], bh, 6)
     receive(5)
+    hh[yhi] = sum_four(hx).astype(BF16)
+    h_all(hh.at[yhi], hh.at[yhi], hh, 7)
+    receive(6)
     blow[x] = (adapter_scale * sum_four(bh)).astype(BF16)
-    for j in range(1, 4):
-        rcopy(blow.at[x], blow.at[x], 8, (l, x_to(j))).start()
-    sent(8, blow.at[pl.ds(0, 3)])
-
-    receive(7)
-    hh[yhi] = sum_four(hx).astype(BF16)
-    for j in range(1, 4):
-        rcopy(hh.at[yhi], hh.at[yhi], 9, (l, h_to(j))).start()
-    sent(9, hh.at[pl.ds(0, 3)])
+    x_all(lambda to: blow.at[x], blow.at[x], blow, 8)
 
     normalizer_scale = 1.0 / math.sqrt(TOKENS)
     receive(8)
@@ -240,30 +235,23 @@
     rcopy(gpack.at[1 - core], gcore, 10, core_peer).start()
     sent(10, gcore)
 
-    receive(9)
+    receive(7)
     hlow[x] = sum_four(hh).astype(BF16)
-    for j in range(1, 4):
-        rcopy(hlow.at[x], hlow.at[x], 11, (l, x_to(j))).start()
-    sent(11, hlow.at[pl.ds(0, 3)])
+    x_all(lambda to: hlow.at[x], hlow.at[x], hlow, 9)
 
     receive(10)
     gsum[...] = (gpack[core].astype(F32) + gcore[...].astype(F32)).astype(BF16)
-
-    def send_gsum(j, c):
-        to = (zy + j) % 16
-        rcopy(gsum.at[to], gz.at[zy], 12, (to * 2 + core, r)).start()
-        return c
-
-    lax.fori_loop(1, 16, send_gsum, 0)
+    zy_all(lambda to: gsum.at[to], gz.at[zy], 12)
     sent(12, gz.at[pl.ds(0, 15)])
     gz[zy] = gsum[zy]
 
-    receive(11)
+    receive(9)
     gradu = (adapter_scale * normalizer_scale) * dot(hlow[...].reshape(ROWS, 128), g_v[...], 0, 0)
     gradu = gradu.astype(BF16)
     stack = jnp.concatenate([gradu[:, 128 * t : 128 * t + 128] for t in range(TU)], axis=0)
     upack[...] = dot(put[...], stack, 1, 0).astype(BF16).reshape(LEARN, PU, 128)
-    learn_all(lambda to: upack.at[to], ured, 13)
+    learn_all(lambda to: upack.at[to], ured.at[l], 13)
+    sent(13, ured.at[pl.ds(0, LEARN - 1)])
     ured[l] = upack[l]
 
     for copy in loads[4:]:
@@ -271,25 +259,12 @@
     receive(12)
     gradient = unpack(jnp.sum(gz[...].astype(F32), axis=0), TD)
     new_p, new_m, new_v = adam(dp_v[...], dm_v[...], dv_v[...], gradient)
-    fsend[0] = pack(new_p[:, :WCOLS], TW, PW)
-    fsend[1] = pack(new_p[:, WCOLS:], TW, PW)
-
-    def send_shard(k, c):
-        to_l, to_r = 2 * r + k // 16, k % 16
-        own = jnp.logical_and(to_l == l, to_r == r)
-
-        @pl.when(jnp.logical_not(own))
-        def _():
-            rcopy(fsend.at[k // 16], fbuf.at[l], 14, (to_l, to_r)).start()
-
-        @pl.when(own)
-        def _():
-            pltpu.make_async_copy(fsend.at[k // 16], fbuf.at[l], recv_sem.at[14]).start()
-
-        return c
-
-    lax.fori_loop(0, 32, send_shard, 0)
-    sent(14, fbuf)
+    fgat[r, pl.ds(0, PW)] = pack(new_p[:, :WCOLS], TW, PW)
+    fgat[r, pl.ds(PW, PW)] = pack(new_p[:, WCOLS:], TW, PW)
+    for j in FAR_FIRST:
+        to = (yhi + j // 4) % 4 * 4 + (x + j % 4) % 4
+        rcopy(fgat.at[r], fgat.at[r], 14, (l, to), roll_sem.at[r]).start()
+    leaving.append((14, fgat.at[pl.ds(0, ROLL - 1)]))
     dpo[...] = new_p
     dmo[...] = new_m
     dvo[...] = new_v
@@ -297,22 +272,38 @@
     receive(13)
     gradient = unpack(jnp.sum(ured[...].astype(F32), axis=0), TU)
     new_p, new_m, new_v = adam(up_v[...], um_v[...], uv_v[...], gradient)
-    unew[l] = pack(new_p, TU, PU)
-    learn_all(lambda to: unew.at[l], unew, 15)
-
+    unew[slot] = pack(new_p, TU, PU)
+    learn_all(lambda to: unew.at[slot], unew.at[slot], 15)
+    sent(15, unew.at[pl.ds(0, LEARN - 1)])
     upo[...] = new_p
     umo[...] = new_m
     uvo[...] = new_v
 
-    receive(14)
+    for j in (0,) + FAR_FIRST[::-1]:
+        piece = (yhi + j // 4) % 4 * 4 + (x + j % 4) % 4
+        if j:
+            drain(fgat.at[piece], roll_sem.at[piece])
+        near, far = fgat.at[piece, pl.ds(core * PW, PW)], fgat.at[piece, pl.ds((1 - core) * PW, PW)]
+        rcopy(far, fbuf.at[l], 16, (2 * piece + 1 - core, r)).start()
+
+        @pl.when(piece != zy)
+        def _():
+            rcopy(near, fbuf.at[l], 16, (2 * piece + core, r)).start()
+
+        @pl.when(piece == zy)
+        def _():
+            pltpu.make_async_copy(near, fbuf.at[l], recv_sem.at[16]).start()
+
+    arriving[16] = fbuf
+    leaving.append((16, fbuf.at[pl.ds(0, LEARN - 1)]))
+
+    receive(16)
     for k in range(2):
         spread = dot(pw[...], fbuf[16 * k : 16 * k + 16].reshape(512, 128), 1, 0).astype(BF16)
         for t in range(TW):
             dnew[64 * k : 64 * k + 64, 128 * t : 128 * t + 128] = spread[64 * t : 64 * t + 64]
     receive(15)
-    spread = dot(pu[...], unew[...].reshape(512, 128), 1, 0).astype(BF16)
-    for t in range(TU):
-        umat[:, 128 * t : 128 * t + 128] = spread[128 * t : 128 * t + 128]
+    unpack_up(unew)
     finish()
 
 
@@ -360,14 +351,14 @@
         out_specs=[vmem] * 9,
         scratch_shapes=[b(ROWS, HID), b(ROWS, OUT)]
         + [pltpu.VMEM(s, F32) for s in small]
-        + [b(LEARN, PU, 128), b(4, NZ, PD, 128), b(RANK, HID)]
+        + [b(LEARN, PU, 128), b(LEARN, PD, 128), b(RANK, HID)]
         + [b(512, 512), b(448, 512), b(512, 448), b(512, 512), b(448, 512)]
         + low
         + low
         + [b(2, 16, PD, 128), b(16, PD, 128), b(16, PD, 128), b(16, PD, 128)]
         + [b(LEARN, PU, 128), b(LEARN, PU, 128), b(LEARN, PU, 128)]
-        + [b(2, PW, 128), b(LEARN, PW, 128)]
-        + [dma((9,)), dma((16,)), dma((16,))],
+        + [b(ROLL, 2 * PW, 128), b(LEARN, PW, 128)]
+        + [dma((9,)), dma((17,)), dma((17,)), dma((ROLL,))],
         compiler_params=pltpu.CompilerParams(
             collective_id=0, has_side_effects=True, vmem_limit_bytes=40 * 2**20
         ),

time: 88.7 us -> 71.3 us (0.80); the launches traced: 88.6 us -> 70.3 us
  Pallas kernels: 87.9 us -> 69.6 us
    pallas_call x1, Pallas kernels: 86.7 us -> 68.4 us  [per_device(): pl.pallas_call(kernel, out_shape=[jax.ShapeDtypeStruct((OUT, WCOLS), BF16...]
where the time goes in v3:
time: 71.3 us; the launch traced here: 70.3 us
  Pallas kernels  69.6 us (98%)
    pallas_call x1, Pallas kernels, per_device(): pl.pallas_call(kernel, out_shape=[jax.ShapeDtypeStruct((OUT, WCOLS), BF16...  68.4 us

profile of v3, /device:TPU:1, one launch (start us, length us, event | category | flops | bytes accessed | tf_op | source)
XLA Modules:
  0.0 70.3 jit_solution(11021333732868608091)
XLA Ops:
  0.6 68.4 %adapter_step.1 = (bf16[512,896]{1,0:T(8,128)(2,1)S(1)}, bf16[128,512]{1,0:T(8,128)(2,1)S(1)}, bf16[128,896]{1,0:T(8,128)(2,1)S(1)}, f32[4,1792]{1,0:T(4,128)S(1...) custom-call(bf16[512,896]{1,0:T(8,128)(2,1)} %w_hbm.1, ...), custom_call_target="tpu_custom_call" | custom-call | flops 1000000000 | bytes 10000000 | tf_op jit(solution)/shard_map/adapter_step/pallas_call | solution.py:342
  69.0 1.3 %merge.1 = (bf16[512,896]{1,0:T(8,128)(2,1)}, f32[4,1792]{1,0:T(4,128)}, f32[4,1792]{1,0:T(4,128)}, f32[4,1792]{1,0:T(4,128)}, f32[4,512]{1,0:T(4,128)}, /*index=5*/f32[4,512]{1,0:T(4,128)}, f32[4,512]{1,0:T(4,128)}) custom-call(bf16[512,896]{1,0:T(8,128)(2,1)S(1)} %get-tuple-element.16.w, bf16[128,512]{1,0:T(8,128)(2,1)S(1)} %get-tuple-element.17.umat, ...), custom_call_target="tpu_custom_call" | custom-call | flops 100000000 | bytes 2000000 | tf_op jit(solution)/shard_map/merge/pallas_call | solution.py:369

commit v4 on v3

--- a/solution.py
+++ b/solution.py
@@ -11,6 +11,7 @@
 BF16, F32 = jnp.bfloat16, jnp.float32
 
 LEARN, ROLL, NX = 32, 16, 4
+ZY_FAR_FIRST = tuple((dz, dp) for dz in (4, 3, 5, 2, 6, 1, 7) for dp in (1, 0)) + ((0, 1),)
 FAR_FIRST = (10, 6, 14, 9, 11, 8, 5, 7, 13, 15, 4, 12, 2, 1, 3)
 RANK, TOKENS, OWN = 128, 20480, 4
 ROWS, HID, OUT, WCOLS = 640, 1792, 512, 896
@@ -36,12 +37,6 @@
     return weights - learning_rate * (update + weight_decay * weights), one_next, two_next
 
 
-def onehot(rows, cols, column_of_row):
-    row = lax.broadcasted_iota(jnp.int32, (rows, cols), 0)
-    col = lax.broadcasted_iota(jnp.int32, (rows, cols), 1)
-    return jnp.where(column_of_row(row) == col, 1.0, 0.0).astype(BF16)
-
-
 def dot(a, b, ca, cb):
     return lax.dot_general(a, b, (((ca,), (cb,)), ((), ())), preferred_element_type=F32)
 
@@ -53,6 +48,26 @@
     return jnp.concatenate(parts, axis=0).astype(BF16)
 
 
+def rank_rows(of_core, tiles):
+    halves = [of_core[c].astype(F32) for c in range(2)]
+    return [
+        jnp.concatenate([h[:, OWN * t : OWN * t + OWN] for h in halves], axis=1)
+        .reshape(RANK, 128)
+        .astype(BF16)
+        for t in range(tiles)
+    ]
+
+
+def packed_rows(grad, core, pad):
+    tiles = [
+        grad[:, 128 * t : 128 * t + 128].reshape(16, 2 * OWN, 128)[:, OWN * core : OWN * core + OWN]
+        for t in range(grad.shape[1] // 128)
+    ]
+    if pad:
+        tiles.append(jnp.zeros((16, pad, 128), F32))
+    return jnp.concatenate(tiles, axis=1).astype(BF16)
+
+
 def unpack(value, tiles):
     return jnp.concatenate([value[OWN * t : OWN * t + OWN] for t in range(tiles)], axis=1)
 
@@ -61,9 +76,9 @@
     w_hbm, x_hbm, g_hbm, dp_hbm, dm_hbm, dv_hbm, up_hbm, um_hbm, uv_hbm,
     w_v, umat, dnew, dpo, dmo, dvo, upo, umo, uvo,
     x_v, g_v, dp_v, dm_v, dv_v, up_v, um_v, uv_v,
-    ubuf, dbuf, dmat, pu, pd, pdt, put, pw,
+    ubuf, dbuf, dmat,
     bpart, bx, bh, blow, hpart, hx, hh, hlow,
-    gpack, gcore, gsum, gz, upack, ured, unew, fgat, fbuf,
+    gpack, gcore, gsum, gz, upack, ucore, usum, uz, unew, fgat, fbuf,
     load_sem, send_sem, recv_sem, roll_sem,
 ):
     l = lax.axis_index("learn")
@@ -73,25 +88,33 @@
     core_peer = (l + 1 - 2 * core, r)
     slot = core * 16 + zy
 
-    barrier = pltpu.get_barrier_semaphore()
-
-    def greet(to):
-        pl.semaphore_signal(barrier, inc=1, device_id=to, device_id_type=MESH)
-
-    for k in range(1, LEARN):
-        greet(((l + k) % LEARN, r))
-    for k in range(1, ROLL):
-        greet((l, (r + k) % ROLL))
-
     loads = []
     for k, (src, dst) in enumerate(
         [(up_hbm, up_v), (dp_hbm, dp_v), (g_hbm, g_v), (x_hbm, x_v), (dm_hbm, dm_v), (dv_hbm, dv_v),
          (um_hbm, um_v), (uv_hbm, uv_v), (w_hbm, w_v)]
     ):
-        copy = pltpu.make_async_copy(src, dst, load_sem.at[k])
+        loads.append(pltpu.make_async_copy(src, dst, load_sem.at[k]))
+    load_up, load_dp, load_g, load_x = loads[:4]
+    load_up.start()
+    load_dp.start()
+
+    barrier = pltpu.get_barrier_semaphore()
+
+    def greet(to):
+        pl.semaphore_signal(barrier, inc=1, device_id=to, device_id_type=MESH)
+
+    def zy_to(dz, dp):
+        return ((zy // 2 + dz) % 8) * 2 + (zy + dp) % 2
+
+    for dz, dp in ZY_FAR_FIRST:
+        greet((zy_to(dz, dp) * 2 + core, r))
+    for j in FAR_FIRST:
+        greet((l, (yhi + j // 4) % 4 * 4 + (x + j % 4) % 4))
+    for dz, dp in ZY_FAR_FIRST:
+        greet((zy_to(dz, dp) * 2 + 1 - core, r))
+    greet(core_peer)
+    for copy in loads[2:]:
         copy.start()
-        loads.append(copy)
-    load_up, load_dp, load_g, load_x = loads[:4]
 
     load_up.wait()
     load_dp.wait()
@@ -124,21 +147,10 @@
         for k, ref in leaving:
             drain(ref, send_sem.at[k])
 
-    def learn_all(src_of, dst, k):
-        def send(j, c):
-            to = (l + j) % LEARN
-            rcopy(src_of(to), dst, k, (to, r)).start()
-            return c
-
-        lax.fori_loop(1, LEARN, send, 0)
-
     def zy_all(src_of, dst, k):
-        def send(j, c):
-            to = (zy + j) % 16
+        for dz, dp in ZY_FAR_FIRST:
+            to = zy_to(dz, dp)
             rcopy(src_of(to), dst, k, (to * 2 + core, r)).start()
-            return c
-
-        lax.fori_loop(1, 16, send, 0)
 
     def x_to(j):
         return yhi * 4 + (x + j) % 4
@@ -162,28 +174,9 @@
     sent(1, dbuf.at[pl.ds(0, 15)])
     half = pl.ds(core * 16, 16)
 
-    pu[...] = onehot(
-        512, 512, lambda a: ((a >> 2) & 1) * 256 + ((a & 127) >> 3) * 16 + (a >> 7) * 4 + (a & 3)
-    )
-    pd[...] = onehot(448, 512, lambda a: ((a & 31) >> 2) * 64 + (a >> 5) * 4 + (a & 3))
-    pdt[...] = onehot(
-        512, 448,
-        lambda a: jnp.where(
-            (a & 63) < 56,
-            ((a & 63) >> 2) * 32 + ((a >> 6) & 3) * 8 + (a >> 8) * 4 + (a & 3),
-            -1,
-        ),
-    )
-    put[...] = onehot(
-        512, 512,
-        lambda a: ((a & 15) >> 2) * 128 + ((a >> 4) & 1) * 64 + (a >> 5) * 4 + (a & 3),
-    )
-    pw[...] = onehot(448, 512, lambda a: ((a & 63) >> 2) * 32 + (a >> 6) * 4 + (a & 3))
-
     def unpack_up(buf):
-        spread = dot(pu[...], buf[...].reshape(512, 128), 1, 0).astype(BF16)
-        for t in range(TU):
-            umat[:, 128 * t : 128 * t + 128] = spread[128 * t : 128 * t + 128]
+        for t, rows in enumerate(rank_rows((buf[:16], buf[16:]), TU)):
+            umat[:, 128 * t : 128 * t + 128] = rows
 
     def sum_four(buf):
         v = buf[...].astype(F32)
@@ -204,10 +197,10 @@
     sent(4, dbuf.at[pl.ds(0, 16)])
     load_x.wait()
     receive(4)
-    for k in range(4):
-        spread = dot(pd[...], dbuf[8 * k : 8 * k + 8].reshape(512, 128), 1, 0).astype(BF16)
-        for t in range(TD):
-            dmat[32 * k : 32 * k + 32, 128 * t : 128 * t + 128] = spread[32 * t : 32 * t + 32]
+    for k in range(0, TD, 4):
+        packed = dbuf[:, OWN * k : OWN * k + 16]
+        for t, rows in enumerate(rank_rows((packed[:16], packed[16:]), min(4, TD - k))):
+            dmat[:, 128 * (k + t) : 128 * (k + t) + 128] = rows
     hpart[...] = dot(x_v[...], dmat[...], 1, 1).astype(BF16).reshape(NX, PART, 128)
     x_all(lambda to: hpart.at[to], hx.at[x], hx, 5)
     hx[x] = hpart[x]
@@ -224,14 +217,12 @@
 
     normalizer_scale = 1.0 / math.sqrt(TOKENS)
     receive(8)
-    grad = (normalizer_scale * dot(blow[...].reshape(ROWS, 128), x_v[...], 0, 0)).astype(BF16)
-    for k in range(4):
-        stack = jnp.concatenate(
-            [grad[32 * k : 32 * k + 32, 128 * t : 128 * t + 128] for t in range(TD)], axis=0
-        )
-        packed = dot(pdt[...], stack, 1, 0).astype(BF16)
-        gpack[0, 4 * k : 4 * k + 4] = packed[:256].reshape(4, PD, 128)
-        gpack[1, 4 * k : 4 * k + 4] = packed[256:].reshape(4, PD, 128)
+    low = blow[...].reshape(ROWS, 128)
+    for k in range(0, TD, 4):
+        tiles = min(4, TD - k)
+        grad = normalizer_scale * dot(low, x_v[:, 128 * k : 128 * (k + tiles)], 0, 0)
+        for c in range(2):
+            gpack[c, :, OWN * k : OWN * k + 16] = packed_rows(grad, c, 16 - OWN * tiles)
     rcopy(gpack.at[1 - core], gcore, 10, core_peer).start()
     sent(10, gcore)
 
@@ -247,12 +238,15 @@
 
     receive(9)
     gradu = (adapter_scale * normalizer_scale) * dot(hlow[...].reshape(ROWS, 128), g_v[...], 0, 0)
-    gradu = gradu.astype(BF16)
-    stack = jnp.concatenate([gradu[:, 128 * t : 128 * t + 128] for t in range(TU)], axis=0)
-    upack[...] = dot(put[...], stack, 1, 0).astype(BF16).reshape(LEARN, PU, 128)
-    learn_all(lambda to: upack.at[to], ured.at[l], 13)
-    sent(13, ured.at[pl.ds(0, LEARN - 1)])
-    ured[l] = upack[l]
+    for c in range(2):
+        upack[c] = packed_rows(gradu, c, 0)
+    rcopy(upack.at[1 - core], ucore, 11, core_peer).start()
+    sent(11, ucore)
+    receive(11)
+    usum[...] = (upack[core].astype(F32) + ucore[...].astype(F32)).astype(BF16)
+    zy_all(lambda to: usum.at[to], uz.at[zy], 13)
+    sent(13, uz.at[pl.ds(0, 15)])
+    uz[zy] = usum[zy]
 
     for copy in loads[4:]:
         copy.wait()
@@ -270,11 +264,11 @@
     dvo[...] = new_v
 
     receive(13)
-    gradient = unpack(jnp.sum(ured[...].astype(F32), axis=0), TU)
+    gradient = unpack(jnp.sum(uz[...].astype(F32), axis=0), TU)
     new_p, new_m, new_v = adam(up_v[...], um_v[...], uv_v[...], gradient)
     unew[slot] = pack(new_p, TU, PU)
-    learn_all(lambda to: unew.at[slot], unew.at[slot], 15)
-    sent(15, unew.at[pl.ds(0, LEARN - 1)])
+    zy_all(lambda to: unew.at[slot], unew.at[slot], 15)
+    sent(15, unew.at[pl.ds(0, 15)])
     upo[...] = new_p
     umo[...] = new_m
     uvo[...] = new_v
@@ -297,12 +291,15 @@
     arriving[16] = fbuf
     leaving.append((16, fbuf.at[pl.ds(0, LEARN - 1)]))
 
+    receive(15)
+    rcopy(unew.at[half], unew.at[half], 17, core_peer).start()
+    sent(17, unew.at[pl.ds(0, 16)])
     receive(16)
-    for k in range(2):
-        spread = dot(pw[...], fbuf[16 * k : 16 * k + 16].reshape(512, 128), 1, 0).astype(BF16)
-        for t in range(TW):
-            dnew[64 * k : 64 * k + 64, 128 * t : 128 * t + 128] = spread[64 * t : 64 * t + 64]
-    receive(15)
+    for k in range(0, TW, 4):
+        packed = fbuf[:, OWN * k : OWN * k + 16].reshape(16, 2, 16, 128)
+        for t, rows in enumerate(rank_rows((packed[:, 0], packed[:, 1]), min(4, TW - k))):
+            dnew[:, 128 * (k + t) : 128 * (k + t) + 128] = rows
+    receive(17)
     unpack_up(unew)
     finish()
 
@@ -352,13 +349,12 @@
         scratch_shapes=[b(ROWS, HID), b(ROWS, OUT)]
         + [pltpu.VMEM(s, F32) for s in small]
         + [b(LEARN, PU, 128), b(LEARN, PD, 128), b(RANK, HID)]
-        + [b(512, 512), b(448, 512), b(512, 448), b(512, 512), b(448, 512)]
         + low
         + low
         + [b(2, 16, PD, 128), b(16, PD, 128), b(16, PD, 128), b(16, PD, 128)]
-        + [b(LEARN, PU, 128), b(LEARN, PU, 128), b(LEARN, PU, 128)]
+        + [b(2, 16, PU, 128), b(16, PU, 128), b(16, PU, 128), b(16, PU, 128), b(LEARN, PU, 128)]
         + [b(ROLL, 2 * PW, 128), b(LEARN, PW, 128)]
-        + [dma((9,)), dma((17,)), dma((17,)), dma((ROLL,))],
+        + [dma((9,)), dma((18,)), dma((18,)), dma((ROLL,))],
         compiler_params=pltpu.CompilerParams(
             collective_id=0, has_side_effects=True, vmem_limit_bytes=40 * 2**20
         ),

time: 71.3 us -> 68.7 us (0.964)
  the two profiles are of different devices: /device:TPU:1 before, /device:TPU:41 now
where the time goes in v4:
time: 68.7 us; the launch traced here: 68.6 us
  Pallas kernels  67.9 us (99%)
    pallas_call x1, Pallas kernels, per_device(): pl.pallas_call(kernel, out_shape=[jax.ShapeDtypeStruct((OUT, WCOLS), BF16...  66.7 us

profile of v4, /device:TPU:41, one launch (start us, length us, event | category | flops | bytes accessed | tf_op | source)
XLA Modules:
  0.0 68.6 jit_solution(14951722925048147953)
XLA Ops:
  0.6 66.7 %adapter_step.1 = (bf16[512,896]{1,0:T(8,128)(2,1)S(1)}, bf16[128,512]{1,0:T(8,128)(2,1)S(1)}, bf16[128,896]{1,0:T(8,128)(2,1)S(1)}, f32[4,1792]{1,0:T(4,128)S(1...) custom-call(bf16[512,896]{1,0:T(8,128)(2,1)} %w_hbm.1, ...), custom_call_target="tpu_custom_call" | custom-call | flops 1000000000 | bytes 10000000 | tf_op jit(solution)/shard_map/adapter_step/pallas_call | solution.py:339
  67.3 1.3 %merge.1 = (bf16[512,896]{1,0:T(8,128)(2,1)}, f32[4,1792]{1,0:T(4,128)}, f32[4,1792]{1,0:T(4,128)}, f32[4,1792]{1,0:T(4,128)}, f32[4,512]{1,0:T(4,128)}, /*index=5*/f32[4,512]{1,0:T(4,128)}, f32[4,512]{1,0:T(4,128)}) custom-call(bf16[512,896]{1,0:T(8,128)(2,1)S(1)} %get-tuple-element.16.w, bf16[128,512]{1,0:T(8,128)(2,1)S(1)} %get-tuple-element.17.umat, ...), custom_call_target="tpu_custom_call" | custom-call | flops 100000000 | bytes 2000000 | tf_op jit(solution)/shard_map/merge/pallas_call | solution.py:365

commit v5 on v4

--- a/solution.py
+++ b/solution.py
@@ -12,7 +12,6 @@
 
 LEARN, ROLL, NX = 32, 16, 4
 ZY_FAR_FIRST = tuple((dz, dp) for dz in (4, 3, 5, 2, 6, 1, 7) for dp in (1, 0)) + ((0, 1),)
-FAR_FIRST = (10, 6, 14, 9, 11, 8, 5, 7, 13, 15, 4, 12, 2, 1, 3)
 RANK, TOKENS, OWN = 128, 20480, 4
 ROWS, HID, OUT, WCOLS = 640, 1792, 512, 896
 PART = ROWS // NX
@@ -103,13 +102,20 @@
     def greet(to):
         pl.semaphore_signal(barrier, inc=1, device_id=to, device_id_type=MESH)
 
+    def x_to(j):
+        return yhi * 4 + (x + j) % 4
+
+    def h_to(j):
+        return ((yhi + j) % 4) * 4 + x
+
     def zy_to(dz, dp):
         return ((zy // 2 + dz) % 8) * 2 + (zy + dp) % 2
 
     for dz, dp in ZY_FAR_FIRST:
         greet((zy_to(dz, dp) * 2 + core, r))
-    for j in FAR_FIRST:
-        greet((l, (yhi + j // 4) % 4 * 4 + (x + j % 4) % 4))
+    for j in (2, 1, 3):
+        greet((l, h_to(j)))
+        greet((l, x_to(j)))
     for dz, dp in ZY_FAR_FIRST:
         greet((zy_to(dz, dp) * 2 + 1 - core, r))
     greet(core_peer)
@@ -120,7 +126,7 @@
     load_dp.wait()
     ubuf[slot] = pack(up_v[...], TU, PU)
     dbuf[slot] = pack(dp_v[...], TD, PD)
-    pl.semaphore_wait(barrier, LEARN + ROLL - 2)
+    pl.semaphore_wait(barrier, LEARN - 1 + 6)
 
     arriving, leaving = {}, []
 
@@ -151,12 +157,6 @@
         for dz, dp in ZY_FAR_FIRST:
             to = zy_to(dz, dp)
             rcopy(src_of(to), dst, k, (to * 2 + core, r)).start()
-
-    def x_to(j):
-        return yhi * 4 + (x + j) % 4
-
-    def h_to(j):
-        return ((yhi + j) % 4) * 4 + x
 
     def x_all(src_of, dst, buf, k):
         for j in (2, 1, 3):
@@ -195,6 +195,9 @@
     receive(1)
     rcopy(dbuf.at[half], dbuf.at[half], 4, core_peer).start()
     sent(4, dbuf.at[pl.ds(0, 16)])
+    receive(3)
+    bh[yhi] = sum_four(bx).astype(BF16)
+    h_all(bh.at[yhi], bh.at[yhi], bh, 6)
     load_x.wait()
     receive(4)
     for k in range(0, TD, 4):
@@ -205,9 +208,6 @@
     x_all(lambda to: hpart.at[to], hx.at[x], hx, 5)
     hx[x] = hpart[x]
 
-    receive(3)
-    bh[yhi] = sum_four(bx).astype(BF16)
-    h_all(bh.at[yhi], bh.at[yhi], bh, 6)
     receive(5)
     hh[yhi] = sum_four(hx).astype(BF16)
     h_all(hh.at[yhi], hh.at[yhi], hh, 7)
@@ -226,15 +226,15 @@
     rcopy(gpack.at[1 - core], gcore, 10, core_peer).start()
     sent(10, gcore)
 
-    receive(7)
-    hlow[x] = sum_four(hh).astype(BF16)
-    x_all(lambda to: hlow.at[x], hlow.at[x], hlow, 9)
-
     receive(10)
     gsum[...] = (gpack[core].astype(F32) + gcore[...].astype(F32)).astype(BF16)
     zy_all(lambda to: gsum.at[to], gz.at[zy], 12)
     sent(12, gz.at[pl.ds(0, 15)])
     gz[zy] = gsum[zy]
+
+    receive(7)
+    hlow[x] = sum_four(hh).astype(BF16)
+    x_all(lambda to: hlow.at[x], hlow.at[x], hlow, 9)
 
     receive(9)
     gradu = (adapter_scale * normalizer_scale) * dot(hlow[...].reshape(ROWS, 128), g_v[...], 0, 0)
@@ -255,13 +255,36 @@
     new_p, new_m, new_v = adam(dp_v[...], dm_v[...], dv_v[...], gradient)
     fgat[r, pl.ds(0, PW)] = pack(new_p[:, :WCOLS], TW, PW)
     fgat[r, pl.ds(PW, PW)] = pack(new_p[:, WCOLS:], TW, PW)
-    for j in FAR_FIRST:
-        to = (yhi + j // 4) % 4 * 4 + (x + j % 4) % 4
-        rcopy(fgat.at[r], fgat.at[r], 14, (l, to), roll_sem.at[r]).start()
+
+    def pass_on(piece, to):
+        rcopy(fgat.at[piece], fgat.at[piece], 14, (l, to), roll_sem.at[piece]).start()
+
+    def arrived(j):
+        piece = (yhi + j // 4) % 4 * 4 + (x + j % 4) % 4
+        if j:
+            drain(fgat.at[piece], roll_sem.at[piece])
+        return piece
+
+    for j in (2, 1, 3):
+        pass_on(r, h_to(j))
+    for j in (2, 1, 3):
+        pass_on(r, x_to(j))
     leaving.append((14, fgat.at[pl.ds(0, ROLL - 1)]))
     dpo[...] = new_p
     dmo[...] = new_m
     dvo[...] = new_v
+
+    def forward(piece):
+        near, far = fgat.at[piece, pl.ds(core * PW, PW)], fgat.at[piece, pl.ds((1 - core) * PW, PW)]
+        rcopy(far, fbuf.at[l], 16, (2 * piece + 1 - core, r)).start()
+
+        @pl.when(piece != zy)
+        def _():
+            rcopy(near, fbuf.at[l], 16, (2 * piece + core, r)).start()
+
+        @pl.when(piece == zy)
+        def _():
+            pltpu.make_async_copy(near, fbuf.at[l], recv_sem.at[16]).start()
 
     receive(13)
     gradient = unpack(jnp.sum(uz[...].astype(F32), axis=0), TU)
@@ -273,21 +296,15 @@
     umo[...] = new_m
     uvo[...] = new_v
 
-    for j in (0,) + FAR_FIRST[::-1]:
-        piece = (yhi + j // 4) % 4 * 4 + (x + j % 4) % 4
-        if j:
-            drain(fgat.at[piece], roll_sem.at[piece])
-        near, far = fgat.at[piece, pl.ds(core * PW, PW)], fgat.at[piece, pl.ds((1 - core) * PW, PW)]
-        rcopy(far, fbuf.at[l], 16, (2 * piece + 1 - core, r)).start()
-
-        @pl.when(piece != zy)
-        def _():
-            rcopy(near, fbuf.at[l], 16, (2 * piece + core, r)).start()
-
-        @pl.when(piece == zy)
-        def _():
-            pltpu.make_async_copy(near, fbuf.at[l], recv_sem.at[16]).start()
-
+    for j in (0, 1, 3, 2):
+        forward(arrived(j))
+    for j in (4, 12, 8):
+        piece = arrived(j)
+        for k in (2, 1, 3):
+            pass_on(piece, x_to(k))
+        forward(piece)
+    for j in (5, 7, 13, 15, 6, 14, 9, 11, 10):
+        forward(arrived(j))
     arriving[16] = fbuf
     leaving.append((16, fbuf.at[pl.ds(0, LEARN - 1)]))
 

time: 68.7 us -> 64.4 us (0.937)
  the two profiles are of different devices: /device:TPU:41 before, /device:TPU:1 now
where the time goes in v5:
time: 64.4 us; the launch traced here: 63.9 us
  Pallas kernels  63.3 us (98%)
    pallas_call x1, Pallas kernels, per_device(): pl.pallas_call(kernel, out_shape=[jax.ShapeDtypeStruct((OUT, WCOLS), BF16...  62 us

profile of v5, /device:TPU:1, one launch (start us, length us, event | category | flops | bytes accessed | tf_op | source)
XLA Modules:
  0.0 63.9 jit_solution(16231860934515892539)
XLA Ops:
  0.6 62.0 %adapter_step.1 = (bf16[512,896]{1,0:T(8,128)(2,1)S(1)}, bf16[128,512]{1,0:T(8,128)(2,1)S(1)}, bf16[128,896]{1,0:T(8,128)(2,1)S(1)}, f32[4,1792]{1,0:T(4,128)S(1...) custom-call(bf16[512,896]{1,0:T(8,128)(2,1)} %w_hbm.1, ...), custom_call_target="tpu_custom_call" | custom-call | flops 1000000000 | bytes 10000000 | tf_op jit(solution)/shard_map/adapter_step/pallas_call | solution.py:356
  62.7 1.3 %merge.1 = (bf16[512,896]{1,0:T(8,128)(2,1)}, f32[4,1792]{1,0:T(4,128)}, f32[4,1792]{1,0:T(4,128)}, f32[4,1792]{1,0:T(4,128)}, f32[4,512]{1,0:T(4,128)}, /*index=5*/f32[4,512]{1,0:T(4,128)}, f32[4,512]{1,0:T(4,128)}) custom-call(bf16[512,896]{1,0:T(8,128)(2,1)S(1)} %get-tuple-element.16.w, bf16[128,512]{1,0:T(8,128)(2,1)S(1)} %get-tuple-element.17.umat, ...), custom_call_target="tpu_custom_call" | custom-call | flops 100000000 | bytes 2000000 | tf_op jit(solution)/shard_map/merge/pallas_call | solution.py:382

commit v6 on v5

--- a/solution.py
+++ b/solution.py
@@ -158,6 +158,17 @@
             to = zy_to(dz, dp)
             rcopy(src_of(to), dst, k, (to * 2 + core, r)).start()
 
+    def part_rows(left, right, part, landing, k):
+        for j in (2, 1, 3, 0):
+            to = (x + j) % 4
+            rows = left[pl.ds(pl.multiple_of(to * PART, PART), PART)]
+            if j:
+                part[to] = dot(rows, right[...], 1, 1).astype(BF16)
+                rcopy(part.at[to], landing.at[x], k, (l, x_to(j))).start()
+            else:
+                landing[to] = dot(rows, right[...], 1, 1).astype(BF16)
+        sent(k, landing.at[pl.ds(0, 3)])
+
     def x_all(src_of, dst, buf, k):
         for j in (2, 1, 3):
             rcopy(src_of((x + j) % 4), dst, k, (l, x_to(j))).start()
@@ -168,8 +179,11 @@
             rcopy(src, dst, k, (l, h_to(j))).start()
         sent(k, buf.at[pl.ds(0, 3)])
 
-    zy_all(lambda to: ubuf.at[slot], ubuf.at[slot], 0)
-    sent(0, ubuf.at[pl.ds(0, 15)])
+    for dz, dp in ZY_FAR_FIRST:
+        for to_core in (core, 1 - core):
+            rcopy(ubuf.at[slot], ubuf.at[slot], 0, (zy_to(dz, dp) * 2 + to_core, r)).start()
+    rcopy(ubuf.at[slot], ubuf.at[slot], 0, core_peer).start()
+    sent(0, ubuf.at[pl.ds(0, LEARN - 1)])
     zy_all(lambda to: dbuf.at[slot], dbuf.at[slot], 1)
     sent(1, dbuf.at[pl.ds(0, 15)])
     half = pl.ds(core * 16, 16)
@@ -182,15 +196,10 @@
         v = buf[...].astype(F32)
         return (v[0] + v[1]) + (v[2] + v[3])
 
+    load_g.wait()
     receive(0)
-    rcopy(ubuf.at[half], ubuf.at[half], 2, core_peer).start()
-    sent(2, ubuf.at[pl.ds(0, 16)])
-    load_g.wait()
-    receive(2)
     unpack_up(ubuf)
-    bpart[...] = dot(g_v[...], umat[...], 1, 1).astype(BF16).reshape(NX, PART, 128)
-    x_all(lambda to: bpart.at[to], bx.at[x], bx, 3)
-    bx[x] = bpart[x]
+    part_rows(g_v, umat, bpart, bx, 3)
 
     receive(1)
     rcopy(dbuf.at[half], dbuf.at[half], 4, core_peer).start()
@@ -204,9 +213,7 @@
         packed = dbuf[:, OWN * k : OWN * k + 16]
         for t, rows in enumerate(rank_rows((packed[:16], packed[16:]), min(4, TD - k))):
             dmat[:, 128 * (k + t) : 128 * (k + t) + 128] = rows
-    hpart[...] = dot(x_v[...], dmat[...], 1, 1).astype(BF16).reshape(NX, PART, 128)
-    x_all(lambda to: hpart.at[to], hx.at[x], hx, 5)
-    hx[x] = hpart[x]
+    part_rows(x_v, dmat, hpart, hx, 5)
 
     receive(5)
     hh[yhi] = sum_four(hx).astype(BF16)

time: 64.4 us -> 64 us (level)
  no operation moved by 1% of the time
where the time goes in v6:
time: 64 us; the launch traced here: 63.6 us
  Pallas kernels  63 us (98%)
  between operations  0.64 us (1%)
    pallas_call x1, Pallas kernels, per_device(): pl.pallas_call(kernel, out_shape=[jax.ShapeDtypeStruct((OUT, WCOLS), BF16...  61.7 us

profile of v6, /device:TPU:1, one launch (start us, length us, event | category | flops | bytes accessed | tf_op | source)
XLA Modules:
  0.0 63.6 jit_solution(10915504541747801784)
XLA Ops:
  0.6 61.7 %adapter_step.1 = (bf16[512,896]{1,0:T(8,128)(2,1)S(1)}, bf16[128,512]{1,0:T(8,128)(2,1)S(1)}, bf16[128,896]{1,0:T(8,128)(2,1)S(1)}, f32[4,1792]{1,0:T(4,128)S(1...) custom-call(bf16[512,896]{1,0:T(8,128)(2,1)} %w_hbm.1, ...), custom_call_target="tpu_custom_call" | custom-call | flops 1000000000 | bytes 10000000 | tf_op jit(solution)/shard_map/adapter_step/pallas_call | solution.py:363
  62.3 1.3 %merge.1 = (bf16[512,896]{1,0:T(8,128)(2,1)}, f32[4,1792]{1,0:T(4,128)}, f32[4,1792]{1,0:T(4,128)}, f32[4,1792]{1,0:T(4,128)}, f32[4,512]{1,0:T(4,128)}, /*index=5*/f32[4,512]{1,0:T(4,128)}, f32[4,512]{1,0:T(4,128)}) custom-call(bf16[512,896]{1,0:T(8,128)(2,1)S(1)} %get-tuple-element.16.w, bf16[128,512]{1,0:T(8,128)(2,1)S(1)} %get-tuple-element.17.umat, ...), custom_call_target="tpu_custom_call" | custom-call | flops 100000000 | bytes 2000000 | tf_op jit(solution)/shard_map/merge/pallas_call | solution.py:389

commit v7 on v6

--- a/solution.py
+++ b/solution.py
@@ -297,8 +297,11 @@
     gradient = unpack(jnp.sum(uz[...].astype(F32), axis=0), TU)
     new_p, new_m, new_v = adam(up_v[...], um_v[...], uv_v[...], gradient)
     unew[slot] = pack(new_p, TU, PU)
-    zy_all(lambda to: unew.at[slot], unew.at[slot], 15)
-    sent(15, unew.at[pl.ds(0, 15)])
+    for dz, dp in ZY_FAR_FIRST:
+        for to_core in (core, 1 - core):
+            rcopy(unew.at[slot], unew.at[slot], 15, (zy_to(dz, dp) * 2 + to_core, r)).start()
+    rcopy(unew.at[slot], unew.at[slot], 15, core_peer).start()
+    sent(15, unew.at[pl.ds(0, LEARN - 1)])
     upo[...] = new_p
     umo[...] = new_m
     uvo[...] = new_v
@@ -315,15 +318,12 @@
     arriving[16] = fbuf
     leaving.append((16, fbuf.at[pl.ds(0, LEARN - 1)]))
 
-    receive(15)
-    rcopy(unew.at[half], unew.at[half], 17, core_peer).start()
-    sent(17, unew.at[pl.ds(0, 16)])
     receive(16)
     for k in range(0, TW, 4):
         packed = fbuf[:, OWN * k : OWN * k + 16].reshape(16, 2, 16, 128)
         for t, rows in enumerate(rank_rows((packed[:, 0], packed[:, 1]), min(4, TW - k))):
             dnew[:, 128 * (k + t) : 128 * (k + t) + 128] = rows
-    receive(17)
+    receive(15)
     unpack_up(unew)
     finish()
 

time: 64 us -> 64.6 us (level)
  Pallas kernels: 63 us -> 63.8 us
    pallas_call x1, Pallas kernels: 61.7 us -> 62.5 us  [per_device(): pl.pallas_call(kernel, out_shape=[jax.ShapeDtypeStruct((OUT, WCOLS), BF16...]
where the time goes in v7:
time: 64.6 us; the launch traced here: 64.4 us
  Pallas kernels  63.8 us (99%)
    pallas_call x1, Pallas kernels, per_device(): pl.pallas_call(kernel, out_shape=[jax.ShapeDtypeStruct((OUT, WCOLS), BF16...  62.5 us

profile of v7, /device:TPU:1, one launch (start us, length us, event | category | flops | bytes accessed | tf_op | source)
XLA Modules:
  0.0 64.4 jit_solution(1862381953563727709)
XLA Ops:
  0.6 62.5 %adapter_step.1 = (bf16[512,896]{1,0:T(8,128)(2,1)S(1)}, bf16[128,512]{1,0:T(8,128)(2,1)S(1)}, bf16[128,896]{1,0:T(8,128)(2,1)S(1)}, f32[4,1792]{1,0:T(4,128)S(1...) custom-call(bf16[512,896]{1,0:T(8,128)(2,1)} %w_hbm.1, ...), custom_call_target="tpu_custom_call" | custom-call | flops 1000000000 | bytes 10000000 | tf_op jit(solution)/shard_map/adapter_step/pallas_call | solution.py:363
  63.1 1.3 %merge.1 = (bf16[512,896]{1,0:T(8,128)(2,1)}, f32[4,1792]{1,0:T(4,128)}, f32[4,1792]{1,0:T(4,128)}, f32[4,1792]{1,0:T(4,128)}, f32[4,512]{1,0:T(4,128)}, /*index=5*/f32[4,512]{1,0:T(4,128)}, f32[4,512]{1,0:T(4,128)}) custom-call(bf16[512,896]{1,0:T(8,128)(2,1)S(1)} %get-tuple-element.16.w, bf16[128,512]{1,0:T(8,128)(2,1)S(1)} %get-tuple-element.17.umat, ...), custom_call_target="tpu_custom_call" | custom-call | flops 100000000 | bytes 2000000 | tf_op jit(solution)/shard_map/merge/pallas_call | solution.py:389
